TPU v7x, 512 devices: a whole 4x4x16 slice. The times are simulated.
512 devices in a mesh: row: 32 (over z, core), col: 16 (over x, y).
Axes of the slice: x: 4, y: 4, z: 16, core: 2. Of those that a mesh axis runs over, the one named last changes fastest.
Arguments:
- slab: float32 [32768, 8192], P('row', 'col'), may hold values from -6 to 6
- reflectors: float32 [32768, 64], P('row', 'col'), as said below
- sketch: float32 [128, 32768], P(None, 'row'), may hold values from -0.5 to 0.5
Outputs:
- updated: float32 [32768, 8192], P('row', 'col')
- coupled: float32 [64, 8192], P(None, 'col')
- sketch_next: float32 [128, 8192], P(None, 'col')
Inputs may be any that keep to these rules, and one draw needn't show every extreme that they name: `reflectors`: each column's squared length is near 2, and columns are correlated.
All inputs are finite; a program needn't handle non-finite values.
Results may differ from a plain program's by a relative error of at most 0.00017.
Values sent between devices are 32-bit elements; how exact they have to be, the bound alone decides.
No kernel may reach another device: no remote copies, remote signals or barrier semaphores. Data moves between devices by JAX's collectives and lax.ppermute only.
A program may use at most 64 MiB of HBM per device.

v0:
```python
import jax
import jax.numpy as jnp
from jax import lax
from jax.sharding import PartitionSpec as P


def matmul(left, right):
    return jnp.dot(left, right, precision=lax.Precision.HIGHEST, preferred_element_type=jnp.float32)


def lower_factor(panel_sketch):
    gram = matmul(panel_sketch.T, panel_sketch)
    return jnp.tril(gram, -1) + jnp.diag(0.5 * jnp.diagonal(gram))


def forward_solve(lower_inverse, values):
    return lax.linalg.triangular_solve(lower_inverse, values, left_side=True, lower=True)


def local(slab, reflectors, sketch):
    total_rows = slab.shape[0] * lax.axis_size("row")
    sketch_rows = sketch.shape[0]
    panel_whole = lax.all_gather(reflectors, "col", axis=1, tiled=True)
    sketch_part = matmul(sketch, panel_whole)
    projection_part = matmul(panel_whole.T, slab)
    panel_sketch = lax.psum(sketch_part, "row")
    lower_inverse = lower_factor(panel_sketch)
    projection = lax.psum(projection_part, "row")
    coupled = forward_solve(lower_inverse, projection)
    updated = slab - matmul(panel_whole, coupled)
    new_sketch = lax.psum(matmul(sketch, updated), "row")
    sketch_next = new_sketch * (sketch_rows / total_rows) ** 0.5
    return (updated, coupled, sketch_next)


def solution(mesh):
    in_specs = (P("row", "col"), P("row", "col"), P(None, "row"))
    out_specs = (P("row", "col"), P(None, "col"), P(None, "col"))
    return jax.shard_map(local, mesh=mesh, in_specs=in_specs, out_specs=out_specs, check_vma=False)
```

profile of v0, /device:TPU:1, one launch (start us, length us, event | category | flops | bytes accessed | tf_op | source)
XLA Modules:
  0.0 452.7 jit_solution(11375034964556703550)
XLA Ops:
  7.2 0.0 copy-start
  7.2 0.0 all-reduce.3.cloned.1.call-start
  7.2 19.8 %all-gather = f32[16,4,1024]{2,1,0:T(4,128)S(1)} all-gather(f32[1,4,1024]{2,1,0:T(4,128)} %bitcast.25), channel_id=1, replica_groups=mesh['row'=32,'col'=16] {'col'}, dimensions={0}, use_global_device_ids=true | all-gather | bytes 278528 | tf_op jit(solution)/shard_map/all_gather | solution.py:23
  27.1 0.1 reshape.19
  27.2 0.0 copy-start.1
  27.2 3.8 fusion.4
  30.9 0.0 all-reduce.3.cloned.1.call-update
  31.0 0.0 all-reduce.5.cloned.1.call-start
  31.0 0.0 copy-done
  31.1 0.7 fusion.2
  31.7 99.0 %psum.21 = f32[128,64]{0,1:T(8,128)S(1)} all-reduce(f32[128,64]{0,1:T(8,128)S(1)} %fusion.2), channel_id=1, replica_groups=mesh['row'=32,'col'=16] {'row'}, use_global_device_ids=true, to_apply=%region_0.0 | all-reduce | flops 8192 | bytes 65536 | tf_op jit(solution)/shard_map/psum | solution.py:26
  130.7 0.2 fusion.3
  130.9 0.8 gather_fusion
  131.7 0.1 select_bitcast_fusion
  131.8 0.0 copy-done.1
  131.8 1.8 copy.12
  133.6 4.9 %custom-call.3 = f32[1,64,64]{1,2,0:T(8,128)S(1)} custom-call(f32[1,64,64]{2,1,0:T(8,128)S(1)} %select_bitcast_fusion), custom_call_target="InvertDiagBlocksLowerTriangular" | custom-call | tf_op jit(solution)/shard_map/triangular_solve | solution.py:17
  138.5 96.2 %all-reduce.3.cloned.1.call-done = f32[64,512]{1,0:T(8,128)} async-done(((f32[64,512]{1,0:T(8,128)}), f32[64,512]{1,0:T(8,128)}) %all-reduce.3.cloned.1.call-update) | async-done | bytes 131088 | tf_op jit(solution)/shard_map/psum | solution.py:28
  234.7 1.2 fusion
  235.9 0.0 copy-start.2
  235.9 3.5 bitcast_subtract_fusion
  239.4 0.0 copy-done.2
  239.4 2.5 convolution_bitcast_fusion
  241.9 0.0 all-reduce.5.cloned.1.call-update
  241.9 1.8 copy.13
  243.8 200.3 %all-reduce.5.cloned.1.call-done = f32[128,512]{0,1:T(8,128)} async-done(((f32[128,512]{0,1:T(8,128)}), f32[128,512]{0,1:T(8,128)}) %all-reduce.5.cloned.1.call-update) | async-done | bytes 262160 | tf_op jit(solution)/shard_map/psum | solution.py:31
  444.0 1.0 broadcast_multiply_fusion
  445.0 0.8 copy.14
  (3 shorter events, 0.0 us)
Async XLA Ops:
  7.2 23.9 %copy-start = (f32[128,1024]{1,0:T(8,128)S(1)}, f32[128,1024]{1,0:T(8,128)}, u32[]{:S(2)}) copy-start(f32[128,1024]{1,0:T(8,128)} %param.5) | copy-start | bytes 1572868
  7.2 227.5 %all-reduce.3.cloned.1.call-start = ((), (), s32[]{:S(2)}) async-start(), calls=%async_computation | async-start | bytes 262144 | tf_op jit(solution)/shard_map/psum | solution.py:28
  27.2 104.7 %copy-start.1 = (f32[1024,512]{1,0:T(8,128)S(1)}, f32[1024,512]{1,0:T(8,128)}, u32[]{:S(2)}) copy-start(f32[1024,512]{1,0:T(8,128)} %param.3) | copy-start | bytes 6291460
  31.0 413.0 %all-reduce.5.cloned.1.call-start = ((), (), s32[]{:S(2)}) async-start(), calls=%async_computation.1 | async-start | bytes 524288 | tf_op jit(solution)/shard_map/psum | solution.py:31
  235.9 3.5 copy-start.2
Sparse Core Ops, SparseCore 0:
  31.1 203.5 all-reduce.2
  242.1 201.9 all-reduce.4
where the time goes:
time: 453 us
  waiting for transfers between devices  296 us (65%)
  blocking collectives  119 us (26%)
  between operations  14.1 us (3%)
  matrix products  11.8 us (3%)
  other arithmetic  5.96 us (1%)
  local copies, waits for them, and re-layouts  5.39 us (1%)
    psum x1, waiting for transfers between devices, local(): new_sketch = lax.psum(matmul(sketch, updated), 'row')  200 us
    psum x1, blocking collectives, local(): panel_sketch = lax.psum(sketch_part, 'row')  99 us
    psum x1, waiting for transfers between devices, local(): projection = lax.psum(projection_part, 'row')  96.2 us
    all_gather x1, blocking collectives, local(): panel_whole = lax.all_gather(reflectors, 'col', axis=1, tiled=True)  19.8 us
    dot_general x5, matrix products, matmul(): jnp.dot(left, right, precision=lax.Precision.HIGHEST, preferred_element_t...  10.6 us
  transfers between devices with their start and end apart: 2, of which 2 were waited for; matrix products, arithmetic and copies ran while one was open for 2% of the time, Pallas kernels for 0%

commit v1 on v0

v1 whole, which is shorter than its diff:
```python
import jax
import jax.numpy as jnp
from jax import lax
from jax.experimental import pallas as pl
from jax.experimental.pallas import tpu as pltpu
from jax.sharding import Mesh, PartitionSpec as P

CORES = 2
NEAR = 2
CHUNKS = 4
LANES = 128
PAIR = 2
LARGE_VMEM = 58 * 1024 * 1024
SMALL_VMEM = 8 * 1024 * 1024
HIGHEST = lax.Precision.HIGHEST
SWAP = [(0, 1), (1, 0)]


def contract(left, right, left_dim, right_dim):
    return lax.dot_general(left, right, (((left_dim,), (right_dim,)), ((), ())), precision=HIGHEST, preferred_element_type=jnp.float32)


def start_loads(source, target, sems):
    step = source.shape[0] // CHUNKS
    copies = []
    for k in range(CHUNKS):
        rows = pl.ds(k * step, step)
        copies.append(pltpu.make_async_copy(source.at[rows, :], target.at[rows, :], sems.at[k]))
        copies[-1].start()
    return copies


def lay_panel(gathered_ref, panel_ref):
    own = gathered_ref.shape[1]
    for k in range(gathered_ref.shape[0]):
        panel_ref[k * own:(k + 1) * own, :] = gathered_ref[k]


def times_slab(left, slab_ref, copies):
    step = slab_ref.shape[0] // CHUNKS
    total = None
    for k in range(CHUNKS):
        copies[k].wait()
        term = contract(left[:, k * step:(k + 1) * step], slab_ref[k * step:(k + 1) * step, :], 1, 0)
        total = term if total is None else total + term
    return total


def sketch_slab_kernel(sketch_ref, slab_hbm, out_ref, slab_ref, sems):
    copies = start_loads(slab_hbm, slab_ref, sems)
    out_ref[...] = times_slab(sketch_ref[...], slab_ref, copies)


def products_kernel(place_ref, gathered_ref, sketch_ref, sketch_slab_ref, slab_hbm, mine_ref, other_ref, slab_ref, panel_ref, blocks_ref, sems):
    copies = start_loads(slab_hbm, slab_ref, sems)
    lay_panel(gathered_ref, panel_ref)
    panel = panel_ref.shape[0]
    sketch_rows = sketch_ref.shape[0]
    blocks = blocks_ref.shape[0]
    folded = panel // blocks
    top = sketch_rows + panel
    panel_sketch = contract(panel_ref[...], sketch_ref[...], 1, 1)
    projection = times_slab(panel_ref[...], slab_ref, copies)
    for j in range(blocks):
        columns = slice(j * LANES, (j + 1) * LANES)
        blocks_ref[j, :sketch_rows, :] = sketch_slab_ref[:, columns]
        blocks_ref[j, sketch_rows:top, :] = projection[:, columns]
        blocks_ref[j, top:, :] = panel_sketch[j * folded:(j + 1) * folded, :]
    half = mine_ref.shape[0]
    core = place_ref[0]
    for out, first in ((other_ref, (1 - core) * half), (mine_ref, core * half)):
        for t in range(half):
            for i in range(out.shape[1]):
                out[t, i] = blocks_ref[first + t, PAIR * i:PAIR * (i + 1), :]


def split_kernel(place_ref, mine_ref, got_ref, keep_ref, send_ref):
    near = place_ref[1]
    send_ref[...] = mine_ref[1 - near] + got_ref[1 - near]
    keep_ref[...] = mine_ref[near] + got_ref[near]


def add_kernel(left_ref, right_ref, out_ref):
    out_ref[...] = left_ref[...] + right_ref[...]


def sum_kernel(parts_ref, out_ref):
    total = parts_ref[0]
    for k in range(1, parts_ref.shape[0]):
        total = total + parts_ref[k]
    for k in range(out_ref.shape[0]):
        out_ref[k] = total


def stack_kernel(first_ref, second_ref, out_ref):
    out_ref[0] = first_ref[...]
    out_ref[1] = second_ref[...]


def update_kernel(scale, place_ref, mine_ref, other_ref, gathered_ref, slab_hbm, updated_hbm, coupled_ref, sketch_next_ref,
                  slab_ref, updated_ref, panel_ref, blocks_ref, in_sems, out_sems):
    loads = start_loads(slab_hbm, slab_ref, in_sems)
    core, near = place_ref[0], place_ref[1]
    sketch_rows, columns = sketch_next_ref.shape
    panel, depth = panel_ref.shape
    step = depth // CHUNKS
    for ref, owner in ((mine_ref, core), (other_ref, 1 - core)):
        for t, side in ((0, near), (1, 1 - near)):
            block = owner * NEAR + side
            for i in range(ref.shape[1]):
                blocks_ref[block, PAIR * i:PAIR * (i + 1), :] = ref[t, i]
    lay_panel(gathered_ref, panel_ref)
    blocks = blocks_ref.shape[0]
    top = sketch_rows + panel
    panel_sketch = jnp.concatenate([blocks_ref[j, top:, :] for j in range(blocks)], axis=0)
    gram = contract(panel_sketch, panel_sketch, 1, 1)
    row = lax.broadcasted_iota(jnp.int32, gram.shape, 0)
    column = lax.broadcasted_iota(jnp.int32, gram.shape, 1)
    strict = jnp.where(row > column, gram, 0.0)
    diagonal = jnp.sum(jnp.where(row == column, gram, 0.0), axis=1, keepdims=True) * 0.5
    inverse = 1.0 / diagonal
    tiles = panel // 8
    values = [jnp.concatenate([blocks_ref[j, sketch_rows + 8 * b:sketch_rows + 8 * b + 8, :] for j in range(blocks)], axis=1)
              for b in range(tiles)]
    scales = [jnp.broadcast_to(inverse[8 * b:8 * b + 8, :], (8, columns)) for b in range(tiles)]
    for i in range(panel):
        b, r = divmod(i, 8)
        solved = values[b][r:r + 1, :] * scales[b][r:r + 1, :]
        for later in range(b, tiles):
            values[later] = values[later] - strict[8 * later:8 * later + 8, i:i + 1] * solved
    coupled = jnp.concatenate([values[b] * scales[b] for b in range(tiles)], axis=0)
    coupled_ref[...] = coupled
    stores = []
    for k in range(CHUNKS):
        rows = pl.ds(k * step, step)
        loads[k].wait()
        moved = contract(panel_ref[:, k * step:(k + 1) * step], coupled, 0, 0)
        updated_ref[k * step:(k + 1) * step, :] = slab_ref[k * step:(k + 1) * step, :] - moved
        stores.append(pltpu.make_async_copy(updated_ref.at[rows, :], updated_hbm.at[rows, :], out_sems.at[k]))
        stores[-1].start()
    correction = contract(panel_sketch, coupled, 0, 0)
    for j in range(blocks):
        lanes = slice(j * LANES, (j + 1) * LANES)
        sketch_next_ref[:, lanes] = (blocks_ref[j, :sketch_rows, :] - correction[:, lanes]) * scale
    for copy in stores:
        copy.wait()


def local(slab, reflectors, sketch):
    depth, columns = slab.shape
    sketch_rows = sketch.shape[0]
    cols, far = lax.axis_size("col"), lax.axis_size("far")
    own = reflectors.shape[1]
    panel = own * cols
    total_rows = depth * far * NEAR * CORES
    blocks = columns // LANES
    place = jnp.stack([lax.axis_index("core"), lax.axis_index("near")]).astype(jnp.int32)
    vmem, smem, hbm = (pl.BlockSpec(memory_space=space) for space in (pltpu.VMEM, pltpu.SMEM, pl.ANY))
    f32 = jnp.float32

    def call(kernel, name, out, in_specs, out_specs=vmem, scratch=(), flops=0, moved=0, grant=LARGE_VMEM):
        shapes = jax.tree.map(lambda shape: jax.ShapeDtypeStruct(shape, f32), out, is_leaf=lambda leaf: isinstance(leaf, tuple))
        return pl.pallas_call(
            kernel, out_shape=shapes, in_specs=in_specs, out_specs=out_specs, scratch_shapes=list(scratch),
            compiler_params=pltpu.CompilerParams(vmem_limit_bytes=grant),
            cost_estimate=pl.CostEstimate(flops=flops, bytes_accessed=moved, transcendentals=0), name=name)

    dma = pltpu.SemaphoreType.DMA((CHUNKS,))
    whole = pltpu.VMEM((depth, columns), f32)
    slab_bytes = depth * columns * 4

    spread = jnp.broadcast_to(reflectors.T[None], (cols, own, depth))
    gathered = lax.all_to_all(spread, "col", 0, 0, tiled=True)
    sketch_slab = call(
        sketch_slab_kernel, "sketch_slab", (sketch_rows, columns), [vmem, hbm], scratch=[whole, dma],
        flops=12 * sketch_rows * depth * columns, moved=slab_bytes)(sketch, slab)

    rows = sketch_rows + panel + panel // blocks
    pairs = rows // PAIR
    half = blocks // CORES
    mine, other = call(
        products_kernel, "products", [(half, pairs, PAIR, LANES)] * 2, [smem, vmem, vmem, vmem, hbm], [vmem, vmem],
        [whole, pltpu.VMEM((panel, depth), f32), pltpu.VMEM((blocks, rows, LANES), f32), dma],
        flops=12 * panel * depth * columns, moved=slab_bytes)(place, gathered, sketch, sketch_slab, slab)

    quarter = (pairs, PAIR, LANES)
    got = lax.ppermute(other, "core", SWAP)
    keep, send = call(split_kernel, "add_cores", [quarter] * 2, [smem, vmem, vmem], [vmem, vmem], grant=SMALL_VMEM)(place, mine, got)
    got = lax.ppermute(send, "near", SWAP)
    parts = call(add_kernel, "add_chips", quarter, [vmem, vmem], grant=SMALL_VMEM)(keep, got).reshape(far, pairs // far, PAIR, LANES)
    parts = lax.all_to_all(parts, "far", 0, 0, tiled=True)
    summed = call(sum_kernel, "sum_parts", parts.shape, [vmem], grant=SMALL_VMEM)(parts)
    first = lax.all_to_all(summed, "far", 0, 0, tiled=True).reshape(quarter)
    second = lax.ppermute(first, "near", SWAP)
    mine = call(stack_kernel, "stack", (2, *quarter), [vmem, vmem], grant=SMALL_VMEM)(first, second)
    other = lax.ppermute(mine, "core", SWAP)

    scale = (sketch_rows / total_rows) ** 0.5
    updated, coupled, sketch_next = call(
        lambda *refs: update_kernel(scale, *refs), "solve_update", [slab.shape, (panel, columns), (sketch_rows, columns)],
        [smem, vmem, vmem, vmem, hbm], [hbm, vmem, vmem],
        [whole, whole, pltpu.VMEM((panel, depth), f32), pltpu.VMEM((blocks, rows, LANES), f32), dma, dma],
        flops=12 * panel * depth * columns, moved=2 * slab_bytes)(place, mine, other, gathered, slab)
    return (updated, coupled, sketch_next)


def solution(mesh):
    split = Mesh(mesh.devices.reshape(-1, NEAR, CORES, mesh.devices.shape[1]), ("far", "near", "core", "col"))
    row = ("far", "near", "core")
    in_specs = (P(row, "col"), P(row, "col"), P(None, row))
    out_specs = (P(row, "col"), P(None, "col"), P(None, "col"))
    return jax.shard_map(local, mesh=split, in_specs=in_specs, out_specs=out_specs, check_vma=False)
```

time: 453 us -> 99.8 us (0.22)
  waiting for transfers between devices: 296 us -> 11.8 us
  blocking collectives: 119 us -> 41.4 us
  starting transfers between devices: 0.08 us -> 24.6 us
  Pallas kernels: 0 us -> 16.2 us
  between operations: 14.1 us -> 0.73 us
  matrix products: 11.8 us -> 0 us
  other arithmetic: 5.96 us -> 0.65 us
    psum x2 -> x0, waiting for transfers between devices: 296 us -> none  [the longest x1 200 us: local(): new_sketch = lax.psum(matmul(sketch, updated), 'row')]
    psum x1 -> x0, blocking collectives: 99 us -> none  [local(): panel_sketch = lax.psum(sketch_part, 'row')]
    all_to_all x0 -> x2, blocking collectives: none -> 41.4 us  [the longest x1 25.7 us: local(): parts = lax.all_to_all(parts, 'far', 0, 0, tiled=True)]
    all_gather x1 -> x0, blocking collectives: 19.8 us -> none  [local(): panel_whole = lax.all_gather(reflectors, 'col', axis=1, tiled=True)]
    ppermute x0 -> x4, starting transfers between devices: none -> 17 us  [the longest x1 6.69 us: local(): other = lax.ppermute(mine, 'core', SWAP)]
    pallas_call x0 -> x7, Pallas kernels: none -> 16.2 us  [the longest x1 6.37 us: local(): call(lambda *refs: update_kernel(scale, *refs), 'solve_update', [slab.sha...]
    dot_general x5 -> x0, matrix products: 10.6 us -> none  [matmul(): jnp.dot(left, right, precision=lax.Precision.HIGHEST, preferred_element_t...]
    ppermute x0 -> x4, waiting for transfers between devices: none -> 9.33 us  [the longest x1 4.15 us: local(): got = lax.ppermute(send, 'near', SWAP)]
  transfers between devices with their start and end apart: 2 -> 5, of which waited for: 2 -> 5; matrix products, arithmetic and copies ran while one was open for 2% -> 1% of each run, Pallas kernels for 0% -> 4%
where the time goes in v1:
time: 99.8 us; the launch traced here: 99.2 us
  blocking collectives  41.4 us (41%)
  starting transfers between devices  24.6 us (25%)
  Pallas kernels  16.2 us (16%)
  waiting for transfers between devices  11.8 us (12%)
  local copies, waits for them, and re-layouts  3.8 us (4%)
    all_to_all x1, blocking collectives, local(): parts = lax.all_to_all(parts, 'far', 0, 0, tiled=True)  25.7 us
    all_to_all x1, blocking collectives, local(): first = lax.all_to_all(summed, 'far', 0, 0, tiled=True).reshape(quarter)  15.8 us
    all_to_all x1, starting transfers between devices, local(): gathered = lax.all_to_all(spread, 'col', 0, 0, tiled=True)  7.58 us
    ppermute x1, starting transfers between devices, local(): other = lax.ppermute(mine, 'core', SWAP)  6.69 us
    pallas_call x1, Pallas kernels, local(): call(lambda *refs: update_kernel(scale, *refs), 'solve_update', [slab.sha...  6.37 us
    ppermute x1, starting transfers between devices, local(): got = lax.ppermute(other, 'core', SWAP)  5.78 us
    pallas_call x1, Pallas kernels, local(): call(products_kernel, 'products', [(half, pairs, PAIR, LANES)] * 2, [smem...  4.79 us
    pallas_call x1, Pallas kernels, local(): call(sketch_slab_kernel, 'sketch_slab', (sketch_rows, columns), [vmem, hb...  4.28 us
  transfers between devices with their start and end apart: 5, of which 5 were waited for; matrix products, arithmetic and copies ran while one was open for 1% of the time, Pallas kernels for 4%

profile of v1, /device:TPU:1, one launch (start us, length us, event | category | flops | bytes accessed | tf_op | source)
XLA Modules:
  0.0 99.2 jit_solution(3760832250761500149)
XLA Ops:
  0.6 1.5 %broadcast_in_dim.2 = f32[16,4,1024]{2,1,0:T(4,128)} broadcast(f32[4,1024]{1,0:T(4,128)} %bitcast.8), dimensions={1,2} | broadcast | bytes 278528 | tf_op jit(solution)/shard_map/broadcast_in_dim | solution.py:172
  2.1 7.6 %all-to-all-start = ((f32[16,4,1024]{2,1,0:T(4,128)}), f32[16,4,1024]{2,1,0:T(4,128)S(1)}, u32[]{:S(2)}, u32[]{:S(2)}) async-start(f32[16,4,1024]{2,1,0:T(4,128)} %broadcast_in_dim.2), calls=%async_computation | async-start | bytes 524288 | tf_op jit(solution)/shard_map/all_to_all | solution.py:173
  9.7 4.3 %sketch_slab.1.sketch_slab_ref = f32[128,512]{1,0:T(8,128)} custom-call(f32[128,1024]{1,0:T(8,128)} %sketch_ref.3, f32[1024,512]{1,0:T(8,128)} %refs_4_.1), custom_call_target="tpu_custom_call" | custom-call | flops 805306368 | bytes 2097152 | tf_op jit(solution)/shard_map/sketch_slab/pallas_call | solution.py:174
  14.0 0.7 pad_add_fusion.place_ref.refs_0_
  14.6 0.0 copy-start.2
  14.6 2.5 %all-to-all-done.gathered_ref.refs_3_ = f32[16,4,1024]{2,1,0:T(4,128)S(1)} async-done(((f32[16,4,1024]{2,1,0:T(4,128)}), f32[16,4,1024]{2,1,0:T(4,128)S(1)}, u32[]{:S(2)}, u32[]{:S(2)}) %all-to-all-start) | async-done | bytes 262176 | tf_op jit(solution)/shard_map/all_to_all | solution.py:173
  17.1 0.0 copy-start.3
  17.1 0.7 copy-done.3
  17.8 4.8 %products.1 = (f32[2,104,2,128]{3,2,1,0:T(2,128)}, f32[2,104,2,128]{3,2,1,0:T(2,128)}) custom-call(s32[2]{0:T(128)} %pad_add_fusion.place_ref.refs_0_, f32[16,4,1024]{2,1,0:T(4,128)} %copy-done.3, f32[128,1024]{1,0:T(8,128)} %sketch_ref.3, f32[128,512]{1,0:T(8,128)} %sketch_slab.1.sketch_slab_ref, f32[1024,512]{1,0:T(8,128)} %refs_4_.1), custom_call_target="tpu_custom_call" | custom-call | flops 402653184 | bytes 2097152 | tf_op jit(solution)/shard_map/products/pallas_call | solution.py:181
  22.6 5.8 %collective-permute-start = (f32[2,104,2,128]{3,2,1,0:T(2,128)}, f32[2,104,2,128]{3,2,1,0:T(2,128)S(1)}, u32[]{:S(2)}, u32[]{:S(2)}) collective-permute-start(f32[2,104,2,128]{3,2,1,0:T(2,128)} %get-tuple-element.8), channel_id=1, source_target_pairs={{0,16},{16,0},{1,17},{17,1},{2,18},{18,2},{3,19},{19,3},{4,20},{20... | collective-permute-start | bytes 638984 | tf_op jit(solution)/shard_map/ppermute | solution.py:187
  28.4 1.3 %collective-permute-done.got_ref = f32[2,104,2,128]{3,2,1,0:T(2,128)S(1)} collective-permute-done((f32[2,104,2,128]{3,2,1,0:T(2,128)}, f32[2,104,2,128]{3,2,1,0:T(2,128)S(1)}, u32[]{:S(2)}, u32[]{:S(2)}) %collective-permute-start) | collective-permute-done | bytes 213024 | tf_op jit(solution)/shard_map/ppermute | solution.py:187
  29.7 0.0 copy-done.2
  29.7 0.0 copy-start.1
  29.7 0.9 copy-done.1
  30.6 0.7 add_cores.1
  31.3 1.9 %collective-permute-start.1 = (f32[104,2,128]{2,1,0:T(2,128)S(1)}, f32[104,2,128]{2,1,0:T(2,128)S(1)}, u32[]{:S(2)}, u32[]{:S(2)}) collective-permute-start(f32[104,2,128]{2,1,0:T(2,128)S(1)} %get-tuple-element.10), channel_id=1, source_target_pairs={{0,32},{32,0},{1,33},{33,1},{2,34},{34,2},{3,35},{35,3},{4,36},{36... | collective-permute-start | bytes 319496 | tf_op jit(solution)/shard_map/ppermute | solution.py:189
  33.2 4.1 %collective-permute-done.1.right_ref = f32[104,2,128]{2,1,0:T(2,128)S(1)} collective-permute-done((f32[104,2,128]{2,1,0:T(2,128)S(1)}, f32[104,2,128]{2,1,0:T(2,128)S(1)}, u32[]{:S(2)}, u32[]{:S(2)}) %collective-permute-start.1) | collective-permute-done | bytes 106528 | tf_op jit(solution)/shard_map/ppermute | solution.py:189
  37.3 0.1 add_chips.1
  37.4 25.7 %all_to_all.15.parts_ref = f32[8,13,2,128]{3,2,1,0:T(2,128)S(1)} all-to-all(f32[8,13,2,128]{3,2,1,0:T(2,128)S(1)} %bitcast.5), channel_id=1, replica_groups=mesh['far'=8,'near'=2,'core'=2,'col'=16] {'far'}, dimensions={0} | all-to-all | bytes 212992 | tf_op jit(solution)/shard_map/all_to_all | solution.py:191
  63.1 15.8 %all_to_all.16 = f32[8,13,2,128]{3,2,1,0:T(2,128)S(1)} all-to-all(f32[8,13,2,128]{3,2,1,0:T(2,128)S(1)} %sum_parts.1), channel_id=1, replica_groups=mesh['far'=8,'near'=2,'core'=2,'col'=16] {'far'}, dimensions={0} | all-to-all | bytes 212992 | tf_op jit(solution)/shard_map/all_to_all | solution.py:193
  78.9 2.6 %collective-permute-start.2 = (f32[104,2,128]{2,1,0:T(2,128)S(1)}, f32[104,2,128]{2,1,0:T(2,128)S(1)}, u32[]{:S(2)}, u32[]{:S(2)}) collective-permute-start(f32[104,2,128]{2,1,0:T(2,128)S(1)} %bitcast.6), channel_id=1, source_target_pairs={{0,32},{32,0},{1,33},{33,1},{2,34},{34,2},{3,35},{35,3},{4,36},{36... | collective-permute-start | bytes 319496 | tf_op jit(solution)/shard_map/ppermute | solution.py:194
  81.5 2.8 %collective-permute-done.2.second_ref = f32[104,2,128]{2,1,0:T(2,128)S(1)} collective-permute-done((f32[104,2,128]{2,1,0:T(2,128)S(1)}, f32[104,2,128]{2,1,0:T(2,128)S(1)}, u32[]{:S(2)}, u32[]{:S(2)}) %collective-permute-start.2) | collective-permute-done | bytes 106528 | tf_op jit(solution)/shard_map/ppermute | solution.py:194
  84.3 0.0 copy-start
  84.4 6.7 %collective-permute-start.3 = (f32[2,104,2,128]{3,2,1,0:T(2,128)S(1)}, f32[2,104,2,128]{3,2,1,0:T(2,128)S(1)}, u32[]{:S(2)}, u32[]{:S(2)}) collective-permute-start(f32[2,104,2,128]{3,2,1,0:T(2,128)S(1)} %stack.13.refs_1_), channel_id=1, source_target_pairs={{0,16},{16,0},{1,17},{17,1},{2,18},{18,2},{3,19},{19,3},{4,20},{20... | collective-permute-start | bytes 638984 | tf_op jit(solution)/shard_map/ppermute | solution.py:196
  91.0 1.1 %collective-permute-done.3.refs_2_ = f32[2,104,2,128]{3,2,1,0:T(2,128)S(1)} collective-permute-done((f32[2,104,2,128]{3,2,1,0:T(2,128)S(1)}, f32[2,104,2,128]{3,2,1,0:T(2,128)S(1)}, u32[]{:S(2)}, u32[]{:S(2)}) %collective-permute-start.3) | collective-permute-done | bytes 213024 | tf_op jit(solution)/shard_map/ppermute | solution.py:196
  92.1 0.0 copy-done
  92.1 0.0 copy-start.4
  92.1 0.7 copy-done.4
  92.8 6.4 %solve_update.1 = (f32[1024,512]{1,0:T(8,128)}, f32[64,512]{1,0:T(8,128)}, f32[128,512]{1,0:T(8,128)}) custom-call(s32[2]{0:T(128)} %pad_add_fusion.place_ref.refs_0_, f32[2,104,2,128]{3,2,1,0:T(2,128)} %copy-done, f32[2,104,2,128]{3,2,1,0:T(2,128)} %copy-done.4, f32[16,4,1024]{2,1,0:T(4,128)} %copy-done.3, f32[1024,512]{1,0:T(8,128)} %refs_4_.1), custom_call_target="tpu_custom_call" | custom-call | flops 402653184 | bytes 4194304 | tf_op jit(solution)/shard_map/solve_update/pallas_call | solution.py:199
  (2 shorter events, 0.1 us)
Async XLA Ops:
  2.1 15.0 %all-to-all-start = ((f32[16,4,1024]{2,1,0:T(4,128)}), f32[16,4,1024]{2,1,0:T(4,128)S(1)}, u32[]{:S(2)}, u32[]{:S(2)}) async-start(f32[16,4,1024]{2,1,0:T(4,128)} %broadcast_in_dim.2), calls=%async_computation | async-start | bytes 524288 | tf_op jit(solution)/shard_map/all_to_all | solution.py:173
  14.6 15.0 %copy-start.2 = (s32[2]{0:T(128)S(1)}, s32[2]{0:T(128)}, u32[]{:S(2)}) copy-start(s32[2]{0:T(128)} %pad_add_fusion.place_ref.refs_0_) | copy-start | bytes 28
  17.1 0.7 copy-start.3
  22.6 7.1 %collective-permute-start = (f32[2,104,2,128]{3,2,1,0:T(2,128)}, f32[2,104,2,128]{3,2,1,0:T(2,128)S(1)}, u32[]{:S(2)}, u32[]{:S(2)}) collective-permute-start(f32[2,104,2,128]{3,2,1,0:T(2,128)} %get-tuple-element.8), channel_id=1, source_target_pairs={{0,16},{16,0},{1,17},{17,1},{2,18},{18,2},{3,19},{19,3},{4,20},{20... | collective-permute-start | bytes 638984 | tf_op jit(solution)/shard_map/ppermute | solution.py:187
  29.7 0.9 copy-start.1
  31.3 6.1 %collective-permute-start.1 = (f32[104,2,128]{2,1,0:T(2,128)S(1)}, f32[104,2,128]{2,1,0:T(2,128)S(1)}, u32[]{:S(2)}, u32[]{:S(2)}) collective-permute-start(f32[104,2,128]{2,1,0:T(2,128)S(1)} %get-tuple-element.10), channel_id=1, source_target_pairs={{0,32},{32,0},{1,33},{33,1},{2,34},{34,2},{3,35},{35,3},{4,36},{36... | collective-permute-start | bytes 319496 | tf_op jit(solution)/shard_map/ppermute | solution.py:189
  78.9 5.4 %collective-permute-start.2 = (f32[104,2,128]{2,1,0:T(2,128)S(1)}, f32[104,2,128]{2,1,0:T(2,128)S(1)}, u32[]{:S(2)}, u32[]{:S(2)}) collective-permute-start(f32[104,2,128]{2,1,0:T(2,128)S(1)} %bitcast.6), channel_id=1, source_target_pairs={{0,32},{32,0},{1,33},{33,1},{2,34},{34,2},{3,35},{35,3},{4,36},{36... | collective-permute-start | bytes 319496 | tf_op jit(solution)/shard_map/ppermute | solution.py:194
  84.3 7.8 %copy-start = (f32[2,104,2,128]{3,2,1,0:T(2,128)}, f32[2,104,2,128]{3,2,1,0:T(2,128)S(1)}, u32[]{:S(2)}) copy-start(f32[2,104,2,128]{3,2,1,0:T(2,128)S(1)} %stack.13.refs_1_) | copy-start | bytes 638980
  84.4 7.8 %collective-permute-start.3 = (f32[2,104,2,128]{3,2,1,0:T(2,128)S(1)}, f32[2,104,2,128]{3,2,1,0:T(2,128)S(1)}, u32[]{:S(2)}, u32[]{:S(2)}) collective-permute-start(f32[2,104,2,128]{3,2,1,0:T(2,128)S(1)} %stack.13.refs_1_), channel_id=1, source_target_pairs={{0,16},{16,0},{1,17},{17,1},{2,18},{18,2},{3,19},{19,3},{4,20},{20... | collective-permute-start | bytes 638984 | tf_op jit(solution)/shard_map/ppermute | solution.py:196
  92.1 0.7 copy-start.4

commit v2 on v1

v2 whole, which is shorter than its diff:
```python
import jax
import jax.numpy as jnp
from jax import lax
from jax.experimental import pallas as pl
from jax.experimental.pallas import tpu as pltpu
from jax.sharding import Mesh, PartitionSpec as P

CORES = 2
CHUNKS = 4
LANES = 128
PAIR = 2
LARGE_VMEM = 52 * 1024 * 1024
SMALL_VMEM = 8 * 1024 * 1024
HIGHEST = lax.Precision.HIGHEST
SWAP = [(0, 1), (1, 0)]


def contract(left, right, left_dim, right_dim, precision=None):
    return lax.dot_general(left, right, (((left_dim,), (right_dim,)), ((), ())), precision=precision, preferred_element_type=jnp.float32)


def parts_of(value):
    high = value.astype(jnp.bfloat16)
    return high, (value - high.astype(jnp.float32)).astype(jnp.bfloat16)


def start_loads(source, target, sems):
    step = source.shape[0] // CHUNKS
    copies = []
    for k in range(CHUNKS):
        rows = pl.ds(k * step, step)
        copies.append(pltpu.make_async_copy(source.at[rows, :], target.at[rows, :], sems.at[k]))
        copies[-1].start()
    return copies


def lay_panel(gathered_ref, panel_ref):
    own = gathered_ref.shape[1]
    for k in range(gathered_ref.shape[0]):
        panel_ref[k * own:(k + 1) * own, :] = gathered_ref[k, :, :panel_ref.shape[1]]


def spread_kernel(own_ref, out_ref):
    for k in range(out_ref.shape[0]):
        out_ref[k] = own_ref[...]


def sketch_slab_kernel(sketch_ref, slab_hbm, out_ref, high_ref, low_ref, slab_ref, sems):
    copies = start_loads(slab_hbm, slab_ref, sems)
    step = slab_ref.shape[0] // CHUNKS
    total = None
    for k in range(CHUNKS):
        copies[k].wait()
        rows = slice(k * step, (k + 1) * step)
        high, low = parts_of(slab_ref[rows, :])
        high_ref[rows, :] = high
        low_ref[rows, :] = low
        term = contract(sketch_ref[:, rows], slab_ref[rows, :], 1, 0, HIGHEST)
        total = term if total is None else total + term
    out_ref[...] = total


def products_kernel(core_ref, gathered_ref, sketch_ref, sketch_slab_ref, high_ref, low_ref, mine_ref, other_ref, panel_ref, blocks_ref):
    lay_panel(gathered_ref, panel_ref)
    panel = panel_ref.shape[0]
    sketch_rows = sketch_ref.shape[0]
    blocks = blocks_ref.shape[0]
    folded = panel // blocks
    top = sketch_rows + panel
    panel_high, panel_low = parts_of(panel_ref[...])
    both = jnp.concatenate([panel_high, panel_low], axis=0)
    sketch_high, sketch_low = parts_of(sketch_ref[...])
    wide = contract(both, sketch_high, 1, 1)
    panel_sketch = wide[:panel] + (wide[panel:] + contract(panel_high, sketch_low, 1, 1))
    wide = contract(both, high_ref[...], 1, 0)
    projection = wide[:panel] + (wide[panel:] + contract(panel_high, low_ref[...], 1, 0))
    for j in range(blocks):
        columns = slice(j * LANES, (j + 1) * LANES)
        blocks_ref[j, :sketch_rows, :] = sketch_slab_ref[:, columns]
        blocks_ref[j, sketch_rows:top, :] = projection[:, columns]
        blocks_ref[j, top:, :] = panel_sketch[j * folded:(j + 1) * folded, :]
    half = blocks // CORES
    pairs = blocks_ref.shape[1] // PAIR
    core = core_ref[0]
    for out, first in ((other_ref, (1 - core) * half), (mine_ref, core * half)):
        for t in range(half):
            for i in range(pairs):
                out[t * pairs + i] = blocks_ref[first + t, PAIR * i:PAIR * (i + 1), :]


def add_kernel(left_ref, right_ref, out_ref):
    out_ref[...] = left_ref[...] + right_ref[...]


def stack_kernel(first, after_ref, gathered_ref, out_ref, panel_ref):
    del after_ref
    own = gathered_ref.shape[1]
    count = out_ref.shape[0]
    for k in range(gathered_ref.shape[0]):
        panel_ref[k * own:(k + 1) * own, :] = gathered_ref[k, :, first:first + count]
    value = panel_ref[...]
    high = value.astype(jnp.bfloat16).astype(jnp.float32)
    out_ref[...] = jnp.concatenate([high, value - high, high], axis=0).T.astype(jnp.bfloat16)


def sum_kernel(parts_ref, after_ref, out_ref):
    del after_ref
    total = parts_ref[0]
    for k in range(1, parts_ref.shape[0]):
        total = total + parts_ref[k]
    for k in range(out_ref.shape[0]):
        out_ref[k] = total


def pass_kernel(value_ref, after_ref, out_ref):
    del after_ref
    out_ref[...] = value_ref[...]


def update_kernel(scale, core_ref, mine_ref, other_ref, top_stack_ref, low_stack_ref, slab_hbm, updated_hbm, coupled_ref, sketch_next_ref,
                  slab_ref, updated_ref, blocks_ref, in_sems, out_sems):
    loads = start_loads(slab_hbm, slab_ref, in_sems)
    core = core_ref[0]
    sketch_rows, columns = sketch_next_ref.shape
    panel = coupled_ref.shape[0]
    blocks = blocks_ref.shape[0]
    half = blocks // CORES
    pairs = blocks_ref.shape[1] // PAIR
    for ref, owner in ((mine_ref, core), (other_ref, 1 - core)):
        for t in range(half):
            for i in range(pairs):
                blocks_ref[owner * half + t, PAIR * i:PAIR * (i + 1), :] = ref[t * pairs + i]
    top = sketch_rows + panel
    panel_sketch = jnp.concatenate([blocks_ref[j, top:, :] for j in range(blocks)], axis=0)
    gram = contract(panel_sketch, panel_sketch, 1, 1, HIGHEST)
    row = lax.broadcasted_iota(jnp.int32, gram.shape, 0)
    column = lax.broadcasted_iota(jnp.int32, gram.shape, 1)
    strict = jnp.where(row > column, gram, 0.0)
    diagonal = jnp.sum(jnp.where(row == column, gram, 0.0), axis=1, keepdims=True) * 0.5
    inverse = 1.0 / diagonal
    tiles = panel // 8
    values = [jnp.concatenate([blocks_ref[j, sketch_rows + 8 * b:sketch_rows + 8 * b + 8, :] for j in range(blocks)], axis=1)
              for b in range(tiles)]
    scales = [jnp.broadcast_to(inverse[8 * b:8 * b + 8, :], (8, columns)) for b in range(tiles)]
    for i in range(panel):
        b, r = divmod(i, 8)
        solved = values[b][r:r + 1, :] * scales[b][r:r + 1, :]
        for later in range(b, tiles):
            values[later] = values[later] - strict[8 * later:8 * later + 8, i:i + 1] * solved
    coupled = jnp.concatenate([values[b] * scales[b] for b in range(tiles)], axis=0)
    coupled_ref[...] = coupled
    high, low = parts_of(coupled)
    right = jnp.concatenate([high, high, low], axis=0)
    step = slab_ref.shape[0] // CHUNKS
    per = CHUNKS // 2
    stores = []
    for k in range(CHUNKS):
        rows = pl.ds(k * step, step)
        stack_ref = (top_stack_ref, low_stack_ref)[k // per]
        moved = contract(stack_ref[(k % per) * step:(k % per + 1) * step, :], right, 1, 0)
        loads[k].wait()
        updated_ref[k * step:(k + 1) * step, :] = slab_ref[k * step:(k + 1) * step, :] - moved
        stores.append(pltpu.make_async_copy(updated_ref.at[rows, :], updated_hbm.at[rows, :], out_sems.at[k]))
        stores[-1].start()
    correction = contract(panel_sketch, coupled, 0, 0, HIGHEST)
    for j in range(blocks):
        lanes = slice(j * LANES, (j + 1) * LANES)
        sketch_next_ref[:, lanes] = (blocks_ref[j, :sketch_rows, :] - correction[:, lanes]) * scale
    for copy in stores:
        copy.wait()


def local(slab, reflectors, sketch):
    depth, columns = slab.shape
    sketch_rows = sketch.shape[0]
    cols, lines = lax.axis_size("col"), lax.axis_size("z")
    own = reflectors.shape[1]
    panel = own * cols
    total_rows = depth * lines * CORES
    blocks = columns // LANES
    core = lax.axis_index("core").astype(jnp.int32).reshape(1)
    vmem, smem, free = (pl.BlockSpec(memory_space=space) for space in (pltpu.VMEM, pltpu.SMEM, pl.ANY))
    f32, bf16 = jnp.float32, jnp.bfloat16

    def call(kernel, name, out, in_specs, out_specs=vmem, scratch=(), flops=0, moved=0, grant=SMALL_VMEM, dtypes=None):
        if isinstance(out, tuple):
            shapes = jax.ShapeDtypeStruct(out, dtypes or f32)
        else:
            shapes = [jax.ShapeDtypeStruct(shape, dtype) for shape, dtype in zip(out, dtypes or [f32] * len(out))]
        return pl.pallas_call(
            kernel, out_shape=shapes, in_specs=in_specs, out_specs=out_specs, scratch_shapes=list(scratch),
            compiler_params=pltpu.CompilerParams(vmem_limit_bytes=grant),
            cost_estimate=pl.CostEstimate(flops=flops, bytes_accessed=moved, transcendentals=0), name=name)

    dma = pltpu.SemaphoreType.DMA((CHUNKS,))
    whole = pltpu.VMEM((depth, columns), f32)
    slab_bytes = depth * columns * 4

    spread = call(spread_kernel, "spread", (cols, own, depth), [vmem])(reflectors.T)
    gathered = lax.all_to_all(spread, "col", 0, 0, tiled=True)
    sketch_slab, high, low = call(
        sketch_slab_kernel, "sketch_slab", [(sketch_rows, columns), slab.shape, slab.shape], [vmem, free], [vmem] * 3, [whole, dma],
        flops=12 * sketch_rows * depth * columns, moved=2 * slab_bytes, grant=LARGE_VMEM, dtypes=[f32, bf16, bf16])(sketch, slab)

    rows = sketch_rows + panel + panel // blocks
    pairs = blocks // CORES * rows // PAIR
    mine, other = call(
        products_kernel, "products", [(pairs, PAIR, LANES)] * 2, [smem] + [vmem] * 5, [vmem, vmem],
        [pltpu.VMEM((panel, depth), f32), pltpu.VMEM((blocks, rows, LANES), f32)],
        flops=6 * panel * depth * columns, moved=slab_bytes, grant=LARGE_VMEM)(core, gathered, sketch, sketch_slab, high, low)

    def stack(first, after):
        count = depth // 2
        return call(
            lambda *refs: stack_kernel(first, *refs), "panel_parts", (count, 3 * panel), [free, vmem],
            scratch=[pltpu.VMEM((panel, count), f32)], flops=100 * panel * count, moved=panel * count * 10, dtypes=bf16)(after, gathered)

    got = lax.ppermute(other, "core", SWAP)
    sums = call(add_kernel, "add_cores", mine.shape, [vmem, vmem])(mine, got).reshape(lines, pairs // lines, PAIR, LANES)
    parts = lax.all_to_all(sums, "z", 0, 0, tiled=True)
    top_stack = stack(0, sums)
    summed = call(sum_kernel, "sum_parts", parts.shape, [vmem, free])(parts, top_stack)
    whole_sums = lax.all_to_all(summed, "z", 0, 0, tiled=True)
    low_stack = stack(depth // 2, summed)
    mine = call(pass_kernel, "pass_on", mine.shape, [vmem, free])(whole_sums.reshape(mine.shape), low_stack)
    other = lax.ppermute(mine, "core", SWAP)

    scale = (sketch_rows / total_rows) ** 0.5
    updated, coupled, sketch_next = call(
        lambda *refs: update_kernel(scale, *refs), "solve_update", [slab.shape, (panel, columns), (sketch_rows, columns)],
        [smem] + [vmem] * 4 + [free], [free, vmem, vmem],
        [whole, whole, pltpu.VMEM((blocks, rows, LANES), f32), dma, dma],
        flops=6 * panel * depth * columns, moved=2 * slab_bytes, grant=LARGE_VMEM)(core, mine, other, top_stack, low_stack, slab)
    return (updated, coupled, sketch_next)


def solution(mesh):
    split = Mesh(mesh.devices.reshape(-1, CORES, mesh.devices.shape[1]), ("z", "core", "col"))
    row = ("z", "core")
    in_specs = (P(row, "col"), P(row, "col"), P(None, row))
    out_specs = (P(row, "col"), P(None, "col"), P(None, "col"))
    return jax.shard_map(local, mesh=split, in_specs=in_specs, out_specs=out_specs, check_vma=False)
```

time: 99.8 us -> 88.2 us (0.88)
  blocking collectives: 41.4 us -> 0 us
  starting transfers between devices: 24.6 us -> 42.6 us
  waiting for transfers between devices: 11.8 us -> 29.1 us
  Pallas kernels: 16.2 us -> 12.4 us
  local copies, waits for them, and re-layouts: 3.8 us -> 2.77 us
    all_to_all x2 -> x0, blocking collectives: 41.4 us -> none  [the longest x1 25.7 us: local(): parts = lax.all_to_all(parts, 'far', 0, 0, tiled=True)]
    all_to_all x0 -> x2, waiting for transfers between devices: none -> 25.4 us  [the longest x1 12.9 us: local(): parts = lax.all_to_all(sums, 'z', 0, 0, tiled=True)]
    all_to_all x0 -> x2, starting transfers between devices: none -> 22.1 us  [the longest x1 13.1 us: local(): parts = lax.all_to_all(sums, 'z', 0, 0, tiled=True)]
    ppermute x2 -> x0, waiting for transfers between devices: 6.98 us -> none  [the longest x1 4.15 us: local(): got = lax.ppermute(send, 'near', SWAP)]
    ppermute x2 -> x0, starting transfers between devices: 4.52 us -> none  [the longest x1 2.59 us: local(): second = lax.ppermute(first, 'near', SWAP)]
    pallas_call x1, Pallas kernels: 6.37 us -> 3.82 us  [local(): call(lambda *refs: update_kernel(scale, *refs), 'solve_update', [slab.sha...]
    broadcast_in_dim x1 -> x0, local copies, waits for them, and re-layouts: 1.47 us -> none  [local(): spread = jnp.broadcast_to(reflectors.T[None], (cols, own, depth))]
    pallas_call x6 -> x8, Pallas kernels: 9.83 us -> 8.56 us  [the longest x1 3.76 us: local(): call(sketch_slab_kernel, 'sketch_slab', [(sketch_rows, columns), slab.sha...]
  transfers between devices with their start and end apart: 5 -> 5, of which waited for: 5 -> 5; matrix products, arithmetic and copies ran while one was open for 1% -> 0% of each run, Pallas kernels for 4% -> 5%
where the time goes in v2:
time: 88.2 us; the launch traced here: 87.6 us
  starting transfers between devices  42.6 us (48%)
  waiting for transfers between devices  29.1 us (33%)
  Pallas kernels  12.4 us (14%)
  local copies, waits for them, and re-layouts  2.77 us (3%)
    all_to_all x1, starting transfers between devices, local(): parts = lax.all_to_all(sums, 'z', 0, 0, tiled=True)  13.1 us
    all_to_all x1, waiting for transfers between devices, local(): parts = lax.all_to_all(sums, 'z', 0, 0, tiled=True)  12.9 us
    all_to_all x1, waiting for transfers between devices, local(): whole_sums = lax.all_to_all(summed, 'z', 0, 0, tiled=True)  12.4 us
    all_to_all x1, starting transfers between devices, local(): whole_sums = lax.all_to_all(summed, 'z', 0, 0, tiled=True)  8.96 us
    all_to_all x1, starting transfers between devices, local(): gathered = lax.all_to_all(spread, 'col', 0, 0, tiled=True)  7.58 us
    ppermute x1, starting transfers between devices, local(): other = lax.ppermute(mine, 'core', SWAP)  7.19 us
    ppermute x1, starting transfers between devices, local(): got = lax.ppermute(other, 'core', SWAP)  5.76 us
    pallas_call x1, Pallas kernels, local(): call(lambda *refs: update_kernel(scale, *refs), 'solve_update', [slab.sha...  3.82 us
  transfers between devices with their start and end apart: 5, of which 5 were waited for; matrix products, arithmetic and copies ran while one was open for 0% of the time, Pallas kernels for 5%

profile of v2, /device:TPU:1, one launch (start us, length us, event | category | flops | bytes accessed | tf_op | source)
XLA Modules:
  0.0 87.6 jit_solution(9533510074764747174)
XLA Ops:
  0.6 0.0 copy-start.2
  0.6 0.0 copy-start.3
  0.7 0.8 copy-done.3
  1.4 0.7 spread.1
  2.1 7.6 %all-to-all-start = ((f32[16,4,1024]{2,1,0:T(4,128)}), f32[16,4,1024]{2,1,0:T(4,128)S(1)}, u32[]{:S(2)}, u32[]{:S(2)}) async-start(f32[16,4,1024]{2,1,0:T(4,128)} %spread.1), calls=%async_computation | async-start | bytes 524288 | tf_op jit(solution)/shard_map/all_to_all | solution.py:200
  9.7 0.0 copy-start.1
  9.7 1.0 %copy-done.1 = f32[128,1024]{1,0:T(8,128)S(1)} copy-done((f32[128,1024]{1,0:T(8,128)S(1)}, f32[128,1024]{1,0:T(8,128)}, u32[]{:S(2)}) %copy-start.1) | copy-done | bytes 524312
  10.8 3.8 %sketch_slab.1 = (f32[128,512]{1,0:T(8,128)S(1)}, bf16[1024,512]{1,0:T(8,128)(2,1)S(1)}, bf16[1024,512]{1,0:T(8,128)(2,1)}) custom-call(f32[128,1024]{1,0:T(8,128)S(1)} %copy-done.1, f32[1024,512]{1,0:T(8,128)} %refs_5_.1), custom_call_target="tpu_custom_call" | custom-call | flops 805306368 | bytes 4194304 | tf_op jit(solution)/shard_map/sketch_slab/pallas_call | solution.py:201
  14.6 0.0 copy-start
  14.6 1.0 %copy-done = bf16[1024,512]{1,0:T(8,128)(2,1)} copy-done((bf16[1024,512]{1,0:T(8,128)(2,1)}, bf16[1024,512]{1,0:T(8,128)(2,1)S(1)}, u32[]{:S(2)}) %copy-start) | copy-done | bytes 1048600
  15.5 1.6 %all-to-all-done.gathered_ref.refs_1_ = f32[16,4,1024]{2,1,0:T(4,128)S(1)} async-done(((f32[16,4,1024]{2,1,0:T(4,128)}), f32[16,4,1024]{2,1,0:T(4,128)S(1)}, u32[]{:S(2)}, u32[]{:S(2)}) %all-to-all-start) | async-done | bytes 262176 | tf_op jit(solution)/shard_map/all_to_all | solution.py:200
  17.1 0.0 copy-done.2
  17.1 2.2 %products.1 = (f32[208,2,128]{2,1,0:T(2,128)S(1)}, f32[208,2,128]{2,1,0:T(2,128)S(1)}) custom-call(s32[1]{0:T(128)} %bitcast.core_ref.refs_0_, f32[16,4,1024]{2,1,0:T(4,128)S(1)} %all-to-all-done.gathered_ref.refs_1_, f32[128,1024]{1,0:T(8,128)S(1)} %copy-done.2, f32[128,512]{1,0:T(8,128)S(1)} %get-tuple-element.8.sketch_slab_ref, ...), custom_call_target="tpu_custom_call" | custom-call | flops 201326592 | bytes 2097152 | tf_op jit(solution)/shard_map/products/pallas_call | solution.py:207
  19.3 5.8 %collective-permute-start = (f32[208,2,128]{2,1,0:T(2,128)S(1)}, f32[208,2,128]{2,1,0:T(2,128)S(1)}, u32[]{:S(2)}, u32[]{:S(2)}) collective-permute-start(f32[208,2,128]{2,1,0:T(2,128)S(1)} %get-tuple-element.12), channel_id=1, source_target_pairs={{0,16},{16,0},{1,17},{17,1},{2,18},{18,2},{3,19},{19,3},{4,20},{20... | collective-permute-start | bytes 638984 | tf_op jit(solution)/shard_map/ppermute | solution.py:218
  25.1 1.1 %collective-permute-done.right_ref = f32[208,2,128]{2,1,0:T(2,128)S(1)} collective-permute-done((f32[208,2,128]{2,1,0:T(2,128)S(1)}, f32[208,2,128]{2,1,0:T(2,128)S(1)}, u32[]{:S(2)}, u32[]{:S(2)}) %collective-permute-start) | collective-permute-done | bytes 213024 | tf_op jit(solution)/shard_map/ppermute | solution.py:218
  26.2 0.8 add_cores.1
  27.0 13.1 %all-to-all-start.1 = ((f32[16,13,2,128]{3,2,1,0:T(2,128)}), f32[16,13,2,128]{3,2,1,0:T(2,128)S(1)}, u32[]{:S(2)}, u32[]{:S(2)}) async-start(f32[16,13,2,128]{3,2,1,0:T(2,128)} %bitcast.2.refs_0_), calls=%async_computation.1 | async-start | bytes 425984 | tf_op jit(solution)/shard_map/all_to_all | solution.py:220
  40.1 0.2 panel_parts.2.after_ref.refs_3_
  40.3 12.9 %all-to-all-done.1.parts_ref = f32[16,13,2,128]{3,2,1,0:T(2,128)S(1)} async-done(((f32[16,13,2,128]{3,2,1,0:T(2,128)}), f32[16,13,2,128]{3,2,1,0:T(2,128)S(1)}, u32[]{:S(2)}, u32[]{:S(2)}) %all-to-all-start.1) | async-done | bytes 213024 | tf_op jit(solution)/shard_map/all_to_all | solution.py:220
  53.2 0.8 sum_parts.1.refs_0_
  54.0 9.0 %all-to-all-start.2 = ((f32[16,13,2,128]{3,2,1,0:T(2,128)}), f32[16,13,2,128]{3,2,1,0:T(2,128)S(1)}, u32[]{:S(2)}, u32[]{:S(2)}) async-start(f32[16,13,2,128]{3,2,1,0:T(2,128)} %sum_parts.1.refs_0_), calls=%async_computation.2 | async-start | bytes 425984 | tf_op jit(solution)/shard_map/all_to_all | solution.py:223
  62.9 0.2 panel_parts.3.after_ref.refs_4_
  63.1 12.4 %all-to-all-done.2 = f32[16,13,2,128]{3,2,1,0:T(2,128)S(1)} async-done(((f32[16,13,2,128]{3,2,1,0:T(2,128)}), f32[16,13,2,128]{3,2,1,0:T(2,128)S(1)}, u32[]{:S(2)}, u32[]{:S(2)}) %all-to-all-start.2) | async-done | bytes 213024 | tf_op jit(solution)/shard_map/all_to_all | solution.py:223
  75.5 7.2 %collective-permute-start.1 = (f32[208,2,128]{2,1,0:T(2,128)S(1)}, f32[208,2,128]{2,1,0:T(2,128)S(1)}, u32[]{:S(2)}, u32[]{:S(2)}) collective-permute-start(f32[208,2,128]{2,1,0:T(2,128)S(1)} %pass_on.1.refs_1_), channel_id=1, source_target_pairs={{0,16},{16,0},{1,17},{17,1},{2,18},{18,2},{3,19},{19,3},{4,20},{20... | collective-permute-start | bytes 638984 | tf_op jit(solution)/shard_map/ppermute | solution.py:226
  82.7 1.1 %collective-permute-done.1.refs_2_ = f32[208,2,128]{2,1,0:T(2,128)S(1)} collective-permute-done((f32[208,2,128]{2,1,0:T(2,128)S(1)}, f32[208,2,128]{2,1,0:T(2,128)S(1)}, u32[]{:S(2)}, u32[]{:S(2)}) %collective-permute-start.1) | collective-permute-done | bytes 213024 | tf_op jit(solution)/shard_map/ppermute | solution.py:226
  83.8 3.8 %solve_update.1 = (f32[1024,512]{1,0:T(8,128)}, f32[64,512]{1,0:T(8,128)}, f32[128,512]{1,0:T(8,128)}) custom-call(s32[1]{0:T(128)} %bitcast.core_ref.refs_0_, f32[208,2,128]{2,1,0:T(2,128)S(1)} %pass_on.1.refs_1_, f32[208,2,128]{2,1,0:T(2,128)S(1)} %collective-permute-done.1.refs_2_, bf16[512,192]{1,0:T(8,128)(2,1)S(1)} %panel_parts.2.after_ref.refs_3_, ...), custom_call_target="tpu_custom_call" | custom-call | flops 201326592 | bytes 4194304 | tf_op jit(solution)/shard_map/solve_update/pallas_call | solution.py:229
  (1 shorter events, 0.0 us)
Async XLA Ops:
  0.6 16.5 %copy-start.2 = (f32[128,1024]{1,0:T(8,128)S(1)}, f32[128,1024]{1,0:T(8,128)}, u32[]{:S(2)}) copy-start(f32[128,1024]{1,0:T(8,128)} %sketch_ref.3) | copy-start | bytes 1572868
  0.6 0.8 copy-start.3
  2.1 15.0 %all-to-all-start = ((f32[16,4,1024]{2,1,0:T(4,128)}), f32[16,4,1024]{2,1,0:T(4,128)S(1)}, u32[]{:S(2)}, u32[]{:S(2)}) async-start(f32[16,4,1024]{2,1,0:T(4,128)} %spread.1), calls=%async_computation | async-start | bytes 524288 | tf_op jit(solution)/shard_map/all_to_all | solution.py:200
  9.7 1.0 %copy-start.1 = (f32[128,1024]{1,0:T(8,128)S(1)}, f32[128,1024]{1,0:T(8,128)}, u32[]{:S(2)}) copy-start(f32[128,1024]{1,0:T(8,128)} %sketch_ref.3) | copy-start | bytes 1572868
  14.6 1.0 %copy-start = (bf16[1024,512]{1,0:T(8,128)(2,1)}, bf16[1024,512]{1,0:T(8,128)(2,1)S(1)}, u32[]{:S(2)}) copy-start(bf16[1024,512]{1,0:T(8,128)(2,1)S(1)} %get-tuple-element.9.high_ref) | copy-start | bytes 3145732
  19.3 6.8 %collective-permute-start = (f32[208,2,128]{2,1,0:T(2,128)S(1)}, f32[208,2,128]{2,1,0:T(2,128)S(1)}, u32[]{:S(2)}, u32[]{:S(2)}) collective-permute-start(f32[208,2,128]{2,1,0:T(2,128)S(1)} %get-tuple-element.12), channel_id=1, source_target_pairs={{0,16},{16,0},{1,17},{17,1},{2,18},{18,2},{3,19},{19,3},{4,20},{20... | collective-permute-start | bytes 638984 | tf_op jit(solution)/shard_map/ppermute | solution.py:218
  27.0 26.2 %all-to-all-start.1 = ((f32[16,13,2,128]{3,2,1,0:T(2,128)}), f32[16,13,2,128]{3,2,1,0:T(2,128)S(1)}, u32[]{:S(2)}, u32[]{:S(2)}) async-start(f32[16,13,2,128]{3,2,1,0:T(2,128)} %bitcast.2.refs_0_), calls=%async_computation.1 | async-start | bytes 425984 | tf_op jit(solution)/shard_map/all_to_all | solution.py:220
  54.0 21.6 %all-to-all-start.2 = ((f32[16,13,2,128]{3,2,1,0:T(2,128)}), f32[16,13,2,128]{3,2,1,0:T(2,128)S(1)}, u32[]{:S(2)}, u32[]{:S(2)}) async-start(f32[16,13,2,128]{3,2,1,0:T(2,128)} %sum_parts.1.refs_0_), calls=%async_computation.2 | async-start | bytes 425984 | tf_op jit(solution)/shard_map/all_to_all | solution.py:223
  75.5 8.3 %collective-permute-start.1 = (f32[208,2,128]{2,1,0:T(2,128)S(1)}, f32[208,2,128]{2,1,0:T(2,128)S(1)}, u32[]{:S(2)}, u32[]{:S(2)}) collective-permute-start(f32[208,2,128]{2,1,0:T(2,128)S(1)} %pass_on.1.refs_1_), channel_id=1, source_target_pairs={{0,16},{16,0},{1,17},{17,1},{2,18},{18,2},{3,19},{19,3},{4,20},{20... | collective-permute-start | bytes 638984 | tf_op jit(solution)/shard_map/ppermute | solution.py:226

commit v3 on v2

v3 whole, which is shorter than its diff:
```python
import jax
import jax.numpy as jnp
from jax import lax
from jax.experimental import pallas as pl
from jax.experimental.pallas import tpu as pltpu
from jax.sharding import Mesh, PartitionSpec as P

CORES = 2
CHUNKS = 4
LANES = 128
PAIR = 2
ALL_VMEM = 60 * 1024 * 1024
LARGE_VMEM = 52 * 1024 * 1024
MIDDLE_VMEM = 16 * 1024 * 1024
SMALL_VMEM = 8 * 1024 * 1024
HIGHEST = lax.Precision.HIGHEST
SWAP = [(0, 1), (1, 0)]


def contract(left, right, left_dim, right_dim, precision=None):
    return lax.dot_general(left, right, (((left_dim,), (right_dim,)), ((), ())), precision=precision, preferred_element_type=jnp.float32)


def parts_of(value):
    high = value.astype(jnp.bfloat16)
    return high, (value - high.astype(jnp.float32)).astype(jnp.bfloat16)


def start_loads(source, target, sems):
    step = source.shape[0] // CHUNKS
    copies = []
    for k in range(CHUNKS):
        rows = pl.ds(k * step, step)
        copies.append(pltpu.make_async_copy(source.at[rows, :], target.at[rows, :], sems.at[k]))
        copies[-1].start()
    return copies


def lay_panel(gathered_ref, panel_ref):
    own = gathered_ref.shape[1]
    for k in range(gathered_ref.shape[0]):
        panel_ref[k * own:(k + 1) * own, :] = gathered_ref[k, :, :panel_ref.shape[1]]


def spread_kernel(own_ref, out_ref):
    for k in range(out_ref.shape[0]):
        out_ref[k] = own_ref[...]


def sketch_slab_kernel(core_ref, sketch_ref, slab_ref, mine_ref, other_ref, high_ref, low_ref, halves_ref):
    step = slab_ref.shape[0] // CHUNKS
    sketch_rows = sketch_ref.shape[0]
    sketch_high, sketch_low = parts_of(sketch_ref[...])
    both = jnp.concatenate([sketch_high, sketch_low], axis=0)
    total = None
    for k in range(CHUNKS):
        rows = slice(k * step, (k + 1) * step)
        high, low = parts_of(slab_ref[rows, :])
        high_ref[rows, :] = high
        low_ref[rows, :] = low
        wide = contract(both[:, rows], high, 1, 0)
        term = wide[:sketch_rows] + (wide[sketch_rows:] + contract(sketch_high[:, rows], low, 1, 0))
        total = term if total is None else total + term
    half = sketch_rows // CORES
    for c in range(CORES):
        halves_ref[c] = total[c * half:(c + 1) * half, :]
    core = core_ref[0]
    for out, owner in ((other_ref, 1 - core), (mine_ref, core)):
        for p in range(out.shape[0]):
            for j in range(out.shape[1]):
                out[p, j] = halves_ref[owner, PAIR * p:PAIR * (p + 1), j * LANES:(j + 1) * LANES]


def products_kernel(is_mine, core_ref, gathered_ref, sketch_ref, high_ref, low_ref, after_ref, out_ref, panel_ref):
    del after_ref
    lay_panel(gathered_ref, panel_ref)
    panel = panel_ref.shape[0]
    count = high_ref.shape[1] // CORES
    blocks = count // LANES
    owner = core_ref[0] if is_mine else 1 - core_ref[0]
    columns = pl.ds(pl.multiple_of(owner * count, count), count)
    share = panel // CORES
    some_high, some_low = parts_of(panel_ref[pl.ds(pl.multiple_of(owner * share, share), share), :])
    some = jnp.concatenate([some_high, some_low], axis=0)
    sketch_high, sketch_low = parts_of(sketch_ref[...])
    wide = contract(some, sketch_high, 1, 1)
    panel_sketch = wide[:share] + (wide[share:] + contract(some_high, sketch_low, 1, 1))
    panel_high, panel_low = parts_of(panel_ref[...])
    both = jnp.concatenate([panel_high, panel_low], axis=0)
    wide = contract(both, high_ref[:, columns], 1, 0)
    projection = wide[:panel] + (wide[panel:] + contract(panel_high, low_ref[:, columns], 1, 0))
    folded = share // blocks
    pairs = (panel + folded) // PAIR
    for t in range(blocks):
        for i in range(panel // PAIR):
            out_ref[t * pairs + i] = projection[PAIR * i:PAIR * (i + 1), t * LANES:(t + 1) * LANES]
        for i in range(folded // PAIR):
            first = t * folded + PAIR * i
            out_ref[t * pairs + panel // PAIR + i] = panel_sketch[first:first + PAIR, :]


def join_kernel(mine_sketch_ref, got_sketch_ref, mine_ref, got_ref, out_ref):
    pieces = out_ref.shape[0]
    tall, blocks = mine_sketch_ref.shape[:2]
    tall = tall // pieces
    per = mine_ref.shape[0] // pieces
    for k in range(pieces):
        for p in range(tall):
            out_ref[k, p * blocks:(p + 1) * blocks] = mine_sketch_ref[k * tall + p] + got_sketch_ref[k * tall + p]
        span = slice(k * per, (k + 1) * per)
        out_ref[k, tall * blocks:] = mine_ref[span] + got_ref[span]


def stack_kernel(first, after_ref, gathered_ref, out_ref, panel_ref):
    del after_ref
    own = gathered_ref.shape[1]
    count = out_ref.shape[0]
    for k in range(gathered_ref.shape[0]):
        panel_ref[k * own:(k + 1) * own, :] = gathered_ref[k, :, first:first + count]
    value = panel_ref[...]
    high = value.astype(jnp.bfloat16).astype(jnp.float32)
    out_ref[...] = jnp.concatenate([high, value - high, high], axis=0).T.astype(jnp.bfloat16)


def sum_kernel(parts_ref, after_ref, out_ref):
    del after_ref
    total = parts_ref[0]
    for k in range(1, parts_ref.shape[0]):
        total = total + parts_ref[k]
    for k in range(out_ref.shape[0]):
        out_ref[k] = total


def pass_kernel(value_ref, after_ref, out_ref):
    del after_ref
    out_ref[...] = value_ref[...]


def update_kernel(scale, core_ref, mine_ref, other_ref, top_stack_ref, low_stack_ref, slab_hbm, updated_hbm, coupled_ref, sketch_next_ref,
                  slab_ref, updated_ref, blocks_ref, halves_ref, in_sems, out_sems):
    loads = start_loads(slab_hbm, slab_ref, in_sems)
    core = core_ref[0]
    sketch_rows, columns = sketch_next_ref.shape
    panel = coupled_ref.shape[0]
    blocks = blocks_ref.shape[0]
    half = blocks // CORES
    pairs = blocks_ref.shape[1] // PAIR
    pieces = mine_ref.shape[0]
    per = half * pairs // pieces
    tall = (mine_ref.shape[1] - per) // blocks
    for ref, owner in ((mine_ref, core), (other_ref, 1 - core)):
        for t in range(half):
            for i in range(pairs):
                k, place = divmod(t * pairs + i, per)
                blocks_ref[owner * half + t, PAIR * i:PAIR * (i + 1), :] = ref[k, tall * blocks + place]
    panel_sketch = jnp.concatenate([blocks_ref[j, panel:, :] for j in range(blocks)], axis=0)
    gram = contract(panel_sketch, panel_sketch, 1, 1, HIGHEST)
    row = lax.broadcasted_iota(jnp.int32, gram.shape, 0)
    column = lax.broadcasted_iota(jnp.int32, gram.shape, 1)
    strict = jnp.where(row > column, gram, 0.0)
    diagonal = jnp.sum(jnp.where(row == column, gram, 0.0), axis=1, keepdims=True) * 0.5
    inverse = 1.0 / diagonal
    tiles = panel // 8
    values = [jnp.concatenate([blocks_ref[j, 8 * b:8 * b + 8, :] for j in range(blocks)], axis=1) for b in range(tiles)]
    scales = [jnp.broadcast_to(inverse[8 * b:8 * b + 8, :], (8, columns)) for b in range(tiles)]
    for i in range(panel):
        b, r = divmod(i, 8)
        solved = values[b][r:r + 1, :] * scales[b][r:r + 1, :]
        for later in range(b, tiles):
            values[later] = values[later] - strict[8 * later:8 * later + 8, i:i + 1] * solved
    coupled = jnp.concatenate([values[b] * scales[b] for b in range(tiles)], axis=0)
    coupled_ref[...] = coupled
    high, low = parts_of(coupled)
    right = jnp.concatenate([high, high, low], axis=0)
    step = slab_ref.shape[0] // CHUNKS
    part = CHUNKS // 2
    stores = []
    for k in range(CHUNKS):
        rows = pl.ds(k * step, step)
        stack_ref = (top_stack_ref, low_stack_ref)[k // part]
        moved = contract(stack_ref[(k % part) * step:(k % part + 1) * step, :], right, 1, 0)
        loads[k].wait()
        updated_ref[k * step:(k + 1) * step, :] = slab_ref[k * step:(k + 1) * step, :] - moved
        stores.append(pltpu.make_async_copy(updated_ref.at[rows, :], updated_hbm.at[rows, :], out_sems.at[k]))
        stores[-1].start()
    count = sketch_rows // CORES
    for ref, owner in ((mine_ref, core), (other_ref, 1 - core)):
        for k in range(pieces):
            for p in range(tall):
                first = (k * tall + p) * PAIR
                for j in range(blocks):
                    halves_ref[owner, first:first + PAIR, j * LANES:(j + 1) * LANES] = ref[k, p * blocks + j]
    correction = contract(panel_sketch, coupled, 0, 0, HIGHEST)
    for c in range(CORES):
        span = slice(c * count, (c + 1) * count)
        sketch_next_ref[span, :] = (halves_ref[c] - correction[span, :]) * scale
    for copy in stores:
        copy.wait()


def local(slab, reflectors, sketch):
    depth, columns = slab.shape
    sketch_rows = sketch.shape[0]
    cols, lines = lax.axis_size("col"), lax.axis_size("z")
    own = reflectors.shape[1]
    panel = own * cols
    total_rows = depth * lines * CORES
    blocks = columns // LANES
    core = lax.axis_index("core").astype(jnp.int32).reshape(1)
    vmem, smem, free = (pl.BlockSpec(memory_space=space) for space in (pltpu.VMEM, pltpu.SMEM, pl.ANY))
    f32, bf16 = jnp.float32, jnp.bfloat16

    def call(kernel, name, out, in_specs, out_specs=vmem, scratch=(), flops=0, moved=0, grant=SMALL_VMEM, dtypes=None):
        if isinstance(out, tuple):
            shapes = jax.ShapeDtypeStruct(out, dtypes or f32)
        else:
            shapes = [jax.ShapeDtypeStruct(shape, dtype) for shape, dtype in zip(out, dtypes or [f32] * len(out))]
        return pl.pallas_call(
            kernel, out_shape=shapes, in_specs=in_specs, out_specs=out_specs, scratch_shapes=list(scratch),
            compiler_params=pltpu.CompilerParams(vmem_limit_bytes=grant),
            cost_estimate=pl.CostEstimate(flops=flops, bytes_accessed=moved, transcendentals=0), name=name)

    dma = pltpu.SemaphoreType.DMA((CHUNKS,))
    whole = pltpu.VMEM((depth, columns), f32)
    slab_bytes = depth * columns * 4

    spread = call(spread_kernel, "spread", (cols, own, depth), [vmem], grant=ALL_VMEM)(reflectors.T)
    gathered = lax.all_to_all(spread, "col", 0, 0, tiled=True)

    half_rows = sketch_rows // CORES
    sketch_half = (half_rows // PAIR, blocks, PAIR, LANES)
    mine_sketch, other_sketch, high, low = call(
        sketch_slab_kernel, "sketch_slab", [sketch_half, sketch_half, slab.shape, slab.shape], [smem, vmem, vmem], [vmem] * 4,
        [pltpu.VMEM((CORES, half_rows, columns), f32)],
        flops=6 * sketch_rows * depth * columns, moved=2 * slab_bytes, grant=MIDDLE_VMEM, dtypes=[f32, f32, bf16, bf16])(core, sketch, slab)
    got_sketch = lax.ppermute(other_sketch, "core", SWAP)

    rows = panel + panel // blocks
    pairs = blocks // CORES * rows // PAIR

    def products(is_mine, after):
        return call(
            lambda *refs: products_kernel(is_mine, *refs), "products", (pairs, PAIR, LANES), [smem] + [vmem] * 4 + [free], vmem,
            [pltpu.VMEM((panel, depth), f32)],
            flops=3 * panel * depth * columns, moved=slab_bytes, grant=MIDDLE_VMEM)(core, gathered, sketch, high, low, after)

    def stack(first, after):
        count = depth // 2
        return call(
            lambda *refs: stack_kernel(first, *refs), "panel_parts", (count, 3 * panel), [free, vmem],
            scratch=[pltpu.VMEM((panel, count), f32)], flops=100 * panel * count, moved=panel * count * 10, dtypes=bf16)(after, gathered)

    other = products(False, core)
    got = lax.ppermute(other, "core", SWAP)
    mine = products(True, other)
    per = pairs // lines
    width = half_rows // PAIR // lines * blocks + per
    sums = call(join_kernel, "join", (lines, width, PAIR, LANES), [vmem] * 4)(mine_sketch, got_sketch, mine, got)
    parts = lax.all_to_all(sums, "z", 0, 0, tiled=True)
    top_stack = stack(0, sums)
    summed = call(sum_kernel, "sum_parts", parts.shape, [vmem, free])(parts, top_stack)
    whole_sums = lax.all_to_all(summed, "z", 0, 0, tiled=True)
    low_stack = stack(depth // 2, summed)
    mine = call(pass_kernel, "pass_on", summed.shape, [vmem, free])(whole_sums, low_stack)
    other = lax.ppermute(mine, "core", SWAP)

    scale = (sketch_rows / total_rows) ** 0.5
    updated, coupled, sketch_next = call(
        lambda *refs: update_kernel(scale, *refs), "solve_update", [slab.shape, (panel, columns), (sketch_rows, columns)],
        [smem] + [vmem] * 4 + [free], [free, vmem, vmem],
        [whole, whole, pltpu.VMEM((blocks, rows, LANES), f32), pltpu.VMEM((CORES, half_rows, columns), f32), dma, dma],
        flops=6 * panel * depth * columns, moved=2 * slab_bytes, grant=LARGE_VMEM)(core, mine, other, top_stack, low_stack, slab)
    return (updated, coupled, sketch_next)


def solution(mesh):
    split = Mesh(mesh.devices.reshape(-1, CORES, mesh.devices.shape[1]), ("z", "core", "col"))
    row = ("z", "core")
    in_specs = (P(row, "col"), P(row, "col"), P(None, row))
    out_specs = (P(row, "col"), P(None, "col"), P(None, "col"))
    return jax.shard_map(local, mesh=split, in_specs=in_specs, out_specs=out_specs, check_vma=False)
```

time: 88.2 us -> 86.4 us (0.980)
  starting transfers between devices: 42.6 us -> 46.6 us
  Pallas kernels: 12.4 us -> 9.01 us
  waiting for transfers between devices: 29.1 us -> 26.8 us
    ppermute x0 -> x1, starting transfers between devices: none -> 4.74 us  [local(): got_sketch = lax.ppermute(other_sketch, 'core', SWAP)]
    pallas_call x5 -> x6, Pallas kernels: 7.5 us -> 4.07 us  [the longest x1 1.5 us: local(): call(spread_kernel, 'spread', (cols, own, depth), [vmem], grant=ALL_VMEM)]
    all_to_all x1, waiting for transfers between devices: 1.6 us -> 0.01 us  [local(): gathered = lax.all_to_all(spread, 'col', 0, 0, tiled=True)]
    unnamed x8 -> x6, local copies, waits for them, and re-layouts: 2.77 us -> 2.63 us
  transfers between devices with their start and end apart: 5 -> 6, of which waited for: 5 -> 4; matrix products, arithmetic and copies ran while one was open for 0% -> 0% of each run, Pallas kernels for 5% -> 2%
where the time goes in v3:
time: 86.4 us; the launch traced here: 85.8 us
  starting transfers between devices  46.6 us (54%)
  waiting for transfers between devices  26.8 us (31%)
  Pallas kernels  9.01 us (10%)
  local copies, waits for them, and re-layouts  2.63 us (3%)
    all_to_all x1, starting transfers between devices, local(): parts = lax.all_to_all(sums, 'z', 0, 0, tiled=True)  13.1 us
    all_to_all x1, waiting for transfers between devices, local(): parts = lax.all_to_all(sums, 'z', 0, 0, tiled=True)  12.9 us
    all_to_all x1, waiting for transfers between devices, local(): whole_sums = lax.all_to_all(summed, 'z', 0, 0, tiled=True)  12.4 us
    all_to_all x1, starting transfers between devices, local(): whole_sums = lax.all_to_all(summed, 'z', 0, 0, tiled=True)  8.94 us
    all_to_all x1, starting transfers between devices, local(): gathered = lax.all_to_all(spread, 'col', 0, 0, tiled=True)  7.58 us
    ppermute x1, starting transfers between devices, local(): other = lax.ppermute(mine, 'core', SWAP)  7.19 us
    ppermute x1, starting transfers between devices, local(): got = lax.ppermute(other, 'core', SWAP)  4.98 us
    ppermute x1, starting transfers between devices, local(): got_sketch = lax.ppermute(other_sketch, 'core', SWAP)  4.74 us
  transfers between devices with their start and end apart: 6, of which 4 were waited for; matrix products, arithmetic and copies ran while one was open for 0% of the time, Pallas kernels for 2%

profile of v3, /device:TPU:1, one launch (start us, length us, event | category | flops | bytes accessed | tf_op | source)
XLA Modules:
  0.0 85.8 jit_solution(6352582839773500762)
XLA Ops:
  0.6 0.0 copy-start.2
  0.6 1.5 %spread.1 = f32[16,4,1024]{2,1,0:T(4,128)} custom-call(f32[4,1024]{1,0:T(4,128)} %bitcast.2), custom_call_target="tpu_custom_call" | custom-call | tf_op jit(solution)/shard_map/spread/pallas_call | solution.py:227
  2.1 7.6 %all-to-all-start = ((f32[16,4,1024]{2,1,0:T(4,128)}), f32[16,4,1024]{2,1,0:T(4,128)S(1)}, u32[]{:S(2)}, u32[]{:S(2)}) async-start(f32[16,4,1024]{2,1,0:T(4,128)} %spread.1), calls=%async_computation | async-start | bytes 524288 | tf_op jit(solution)/shard_map/all_to_all | solution.py:228
  9.7 0.0 copy-start
  9.7 1.6 %copy-done = f32[1024,512]{1,0:T(8,128)S(1)} copy-done((f32[1024,512]{1,0:T(8,128)S(1)}, f32[1024,512]{1,0:T(8,128)}, u32[]{:S(2)}) %copy-start) | copy-done | bytes 2097176
  11.3 0.0 copy-start.1
  11.3 1.0 %copy-done.1 = f32[128,1024]{1,0:T(8,128)S(1)} copy-done((f32[128,1024]{1,0:T(8,128)S(1)}, f32[128,1024]{1,0:T(8,128)}, u32[]{:S(2)}) %copy-start.1) | copy-done | bytes 524312
  12.4 0.8 sketch_slab.1
  13.2 4.7 %collective-permute-start = (f32[32,4,2,128]{3,2,1,0:T(2,128)S(1)}, f32[32,4,2,128]{3,2,1,0:T(2,128)S(1)}, u32[]{:S(2)}, u32[]{:S(2)}) collective-permute-start(f32[32,4,2,128]{3,2,1,0:T(2,128)S(1)} %get-tuple-element.8), channel_id=1, source_target_pairs={{0,16},{16,0},{1,17},{17,1},{2,18},{18,2},{3,19},{19,3},{4,20},{20... | collective-permute-start | bytes 393224 | tf_op jit(solution)/shard_map/ppermute | solution.py:236
  17.9 0.0 all-to-all-done.refs_1_
  17.9 0.0 copy-done.2
  18.0 0.5 products.2.refs_5_
  18.4 5.0 %collective-permute-start.1 = (f32[80,2,128]{2,1,0:T(2,128)S(1)}, f32[80,2,128]{2,1,0:T(2,128)S(1)}, u32[]{:S(2)}, u32[]{:S(2)}) collective-permute-start(f32[80,2,128]{2,1,0:T(2,128)S(1)} %products.2.refs_5_), channel_id=1, source_target_pairs={{0,16},{16,0},{1,17},{17,1},{2,18},{18,2},{3,19},{19,3},{4,20},{20... | collective-permute-start | bytes 245768 | tf_op jit(solution)/shard_map/ppermute | solution.py:254
  23.4 0.5 products.3.mine_ref
  23.9 0.0 collective-permute-done.got_sketch_ref
  23.9 0.4 collective-permute-done.1.got_ref
  24.3 0.8 join.1.refs_0_
  25.1 13.1 %all-to-all-start.1 = ((f32[16,13,2,128]{3,2,1,0:T(2,128)}), f32[16,13,2,128]{3,2,1,0:T(2,128)S(1)}, u32[]{:S(2)}, u32[]{:S(2)}) async-start(f32[16,13,2,128]{3,2,1,0:T(2,128)} %join.1.refs_0_), calls=%async_computation.1 | async-start | bytes 425984 | tf_op jit(solution)/shard_map/all_to_all | solution.py:259
  38.2 0.2 panel_parts.2.after_ref.refs_3_
  38.4 12.9 %all-to-all-done.1.parts_ref = f32[16,13,2,128]{3,2,1,0:T(2,128)S(1)} async-done(((f32[16,13,2,128]{3,2,1,0:T(2,128)}), f32[16,13,2,128]{3,2,1,0:T(2,128)S(1)}, u32[]{:S(2)}, u32[]{:S(2)}) %all-to-all-start.1) | async-done | bytes 213024 | tf_op jit(solution)/shard_map/all_to_all | solution.py:259
  51.3 0.8 sum_parts.1.refs_0_
  52.1 8.9 %all-to-all-start.2 = ((f32[16,13,2,128]{3,2,1,0:T(2,128)}), f32[16,13,2,128]{3,2,1,0:T(2,128)S(1)}, u32[]{:S(2)}, u32[]{:S(2)}) async-start(f32[16,13,2,128]{3,2,1,0:T(2,128)} %sum_parts.1.refs_0_), calls=%async_computation.2 | async-start | bytes 425984 | tf_op jit(solution)/shard_map/all_to_all | solution.py:262
  61.0 0.2 panel_parts.3.after_ref.refs_4_
  61.2 12.4 %all-to-all-done.2.value_ref = f32[16,13,2,128]{3,2,1,0:T(2,128)S(1)} async-done(((f32[16,13,2,128]{3,2,1,0:T(2,128)}), f32[16,13,2,128]{3,2,1,0:T(2,128)S(1)}, u32[]{:S(2)}, u32[]{:S(2)}) %all-to-all-start.2) | async-done | bytes 213024 | tf_op jit(solution)/shard_map/all_to_all | solution.py:262
  73.6 7.2 %collective-permute-start.2 = (f32[16,13,2,128]{3,2,1,0:T(2,128)S(1)}, f32[16,13,2,128]{3,2,1,0:T(2,128)S(1)}, u32[]{:S(2)}, u32[]{:S(2)}) collective-permute-start(f32[16,13,2,128]{3,2,1,0:T(2,128)S(1)} %pass_on.1.refs_1_), channel_id=1, source_target_pairs={{0,16},{16,0},{1,17},{17,1},{2,18},{18,2},{3,19},{19,3},{4,20},{20... | collective-permute-start | bytes 638984 | tf_op jit(solution)/shard_map/ppermute | solution.py:265
  80.8 1.1 %collective-permute-done.2.refs_2_ = f32[16,13,2,128]{3,2,1,0:T(2,128)S(1)} collective-permute-done((f32[16,13,2,128]{3,2,1,0:T(2,128)S(1)}, f32[16,13,2,128]{3,2,1,0:T(2,128)S(1)}, u32[]{:S(2)}, u32[]{:S(2)}) %collective-permute-start.2) | collective-permute-done | bytes 213024 | tf_op jit(solution)/shard_map/ppermute | solution.py:265
  81.9 3.9 %solve_update.1 = (f32[1024,512]{1,0:T(8,128)}, f32[64,512]{1,0:T(8,128)}, f32[128,512]{1,0:T(8,128)}) custom-call(s32[1]{0:T(128)} %bitcast.core_ref.refs_0_.refs_5_, f32[16,13,2,128]{3,2,1,0:T(2,128)S(1)} %pass_on.1.refs_1_, f32[16,13,2,128]{3,2,1,0:T(2,128)S(1)} %collective-permute-done.2.refs_2_, bf16[512,192]{1,0:T(8,128)(2,1)S(1)} %panel_parts.2.after_ref.refs_3_, ...), custom_call_target="tpu_custom_call" | custom-call | flops 201326592 | bytes 4194304 | tf_op jit(solution)/shard_map/solve_update/pallas_call | solution.py:268
  (1 shorter events, 0.0 us)
Async XLA Ops:
  0.6 17.3 %copy-start.2 = (f32[128,1024]{1,0:T(8,128)S(1)}, f32[128,1024]{1,0:T(8,128)}, u32[]{:S(2)}) copy-start(f32[128,1024]{1,0:T(8,128)} %refs_2_.3) | copy-start | bytes 1572868
  2.1 15.8 %all-to-all-start = ((f32[16,4,1024]{2,1,0:T(4,128)}), f32[16,4,1024]{2,1,0:T(4,128)S(1)}, u32[]{:S(2)}, u32[]{:S(2)}) async-start(f32[16,4,1024]{2,1,0:T(4,128)} %spread.1), calls=%async_computation | async-start | bytes 524288 | tf_op jit(solution)/shard_map/all_to_all | solution.py:228
  9.7 1.6 %copy-start = (f32[1024,512]{1,0:T(8,128)S(1)}, f32[1024,512]{1,0:T(8,128)}, u32[]{:S(2)}) copy-start(f32[1024,512]{1,0:T(8,128)} %refs_5_.1) | copy-start | bytes 6291460
  11.3 1.0 %copy-start.1 = (f32[128,1024]{1,0:T(8,128)S(1)}, f32[128,1024]{1,0:T(8,128)}, u32[]{:S(2)}) copy-start(f32[128,1024]{1,0:T(8,128)} %refs_2_.3) | copy-start | bytes 1572868
  13.2 10.7 %collective-permute-start = (f32[32,4,2,128]{3,2,1,0:T(2,128)S(1)}, f32[32,4,2,128]{3,2,1,0:T(2,128)S(1)}, u32[]{:S(2)}, u32[]{:S(2)}) collective-permute-start(f32[32,4,2,128]{3,2,1,0:T(2,128)S(1)} %get-tuple-element.8), channel_id=1, source_target_pairs={{0,16},{16,0},{1,17},{17,1},{2,18},{18,2},{3,19},{19,3},{4,20},{20... | collective-permute-start | bytes 393224 | tf_op jit(solution)/shard_map/ppermute | solution.py:236
  18.4 5.9 %collective-permute-start.1 = (f32[80,2,128]{2,1,0:T(2,128)S(1)}, f32[80,2,128]{2,1,0:T(2,128)S(1)}, u32[]{:S(2)}, u32[]{:S(2)}) collective-permute-start(f32[80,2,128]{2,1,0:T(2,128)S(1)} %products.2.refs_5_), channel_id=1, source_target_pairs={{0,16},{16,0},{1,17},{17,1},{2,18},{18,2},{3,19},{19,3},{4,20},{20... | collective-permute-start | bytes 245768 | tf_op jit(solution)/shard_map/ppermute | solution.py:254
  25.1 26.2 %all-to-all-start.1 = ((f32[16,13,2,128]{3,2,1,0:T(2,128)}), f32[16,13,2,128]{3,2,1,0:T(2,128)S(1)}, u32[]{:S(2)}, u32[]{:S(2)}) async-start(f32[16,13,2,128]{3,2,1,0:T(2,128)} %join.1.refs_0_), calls=%async_computation.1 | async-start | bytes 425984 | tf_op jit(solution)/shard_map/all_to_all | solution.py:259
  52.1 21.5 %all-to-all-start.2 = ((f32[16,13,2,128]{3,2,1,0:T(2,128)}), f32[16,13,2,128]{3,2,1,0:T(2,128)S(1)}, u32[]{:S(2)}, u32[]{:S(2)}) async-start(f32[16,13,2,128]{3,2,1,0:T(2,128)} %sum_parts.1.refs_0_), calls=%async_computation.2 | async-start | bytes 425984 | tf_op jit(solution)/shard_map/all_to_all | solution.py:262
  73.6 8.3 %collective-permute-start.2 = (f32[16,13,2,128]{3,2,1,0:T(2,128)S(1)}, f32[16,13,2,128]{3,2,1,0:T(2,128)S(1)}, u32[]{:S(2)}, u32[]{:S(2)}) collective-permute-start(f32[16,13,2,128]{3,2,1,0:T(2,128)S(1)} %pass_on.1.refs_1_), channel_id=1, source_target_pairs={{0,16},{16,0},{1,17},{17,1},{2,18},{18,2},{3,19},{19,3},{4,20},{20... | collective-permute-start | bytes 638984 | tf_op jit(solution)/shard_map/ppermute | solution.py:265

commit v4 on v3

--- a/solution.py
+++ b/solution.py
@@ -6,6 +6,7 @@
 from jax.sharding import Mesh, PartitionSpec as P
 
 CORES = 2
+NEAR = 2
 CHUNKS = 4
 LANES = 128
 PAIR = 2
@@ -69,6 +70,13 @@
         for p in range(out.shape[0]):
             for j in range(out.shape[1]):
                 out[p, j] = halves_ref[owner, PAIR * p:PAIR * (p + 1), j * LANES:(j + 1) * LANES]
+
+
+def split_kernel(near_ref, mine_ref, got_ref, keep_ref, send_ref):
+    near, count = near_ref[0], keep_ref.shape[0]
+    for out, side in ((send_ref, 1 - near), (keep_ref, near)):
+        span = pl.ds(side * count, count)
+        out[...] = mine_ref[span] + got_ref[span]
 
 
 def products_kernel(is_mine, core_ref, gathered_ref, sketch_ref, high_ref, low_ref, after_ref, out_ref, panel_ref):
@@ -99,44 +107,40 @@
             out_ref[t * pairs + panel // PAIR + i] = panel_sketch[first:first + PAIR, :]
 
 
-def join_kernel(mine_sketch_ref, got_sketch_ref, mine_ref, got_ref, out_ref):
-    pieces = out_ref.shape[0]
-    tall, blocks = mine_sketch_ref.shape[:2]
-    tall = tall // pieces
+def join_kernel(keep_ref, got_sketch_ref, mine_ref, got_ref, after_ref, out_ref):
+    del after_ref
+    pieces, width = keep_ref.shape[:2]
     per = mine_ref.shape[0] // pieces
     for k in range(pieces):
-        for p in range(tall):
-            out_ref[k, p * blocks:(p + 1) * blocks] = mine_sketch_ref[k * tall + p] + got_sketch_ref[k * tall + p]
+        out_ref[k, :width] = keep_ref[k] + got_sketch_ref[k]
         span = slice(k * per, (k + 1) * per)
-        out_ref[k, tall * blocks:] = mine_ref[span] + got_ref[span]
-
-
-def stack_kernel(first, after_ref, gathered_ref, out_ref, panel_ref):
+        out_ref[k, width:] = mine_ref[span] + got_ref[span]
+
+
+def stack_kernel(after_ref, gathered_ref, out_ref, panel_ref):
     del after_ref
-    own = gathered_ref.shape[1]
-    count = out_ref.shape[0]
-    for k in range(gathered_ref.shape[0]):
-        panel_ref[k * own:(k + 1) * own, :] = gathered_ref[k, :, first:first + count]
-    value = panel_ref[...]
-    high = value.astype(jnp.bfloat16).astype(jnp.float32)
-    out_ref[...] = jnp.concatenate([high, value - high, high], axis=0).T.astype(jnp.bfloat16)
-
-
-def sum_kernel(parts_ref, after_ref, out_ref):
-    del after_ref
-    total = parts_ref[0]
-    for k in range(1, parts_ref.shape[0]):
-        total = total + parts_ref[k]
+    lay_panel(gathered_ref, panel_ref)
+    step = panel_ref.shape[1] // CHUNKS
+    for k in range(CHUNKS):
+        value = panel_ref[:, k * step:(k + 1) * step]
+        high = value.astype(jnp.bfloat16).astype(jnp.float32)
+        out_ref[k * step:(k + 1) * step, :] = jnp.concatenate([high, value - high, high], axis=0).T.astype(jnp.bfloat16)
+
+
+def sum_kernel(width, parts_ref, out_ref):
+    sides = [parts_ref[n] for n in range(NEAR)]
+    for k in range(NEAR, parts_ref.shape[0]):
+        sides[k % NEAR] = sides[k % NEAR] + parts_ref[k]
+    total = sides[0]
+    for side in sides[1:]:
+        total = total + side
     for k in range(out_ref.shape[0]):
-        out_ref[k] = total
-
-
-def pass_kernel(value_ref, after_ref, out_ref):
-    del after_ref
-    out_ref[...] = value_ref[...]
-
-
-def update_kernel(scale, core_ref, mine_ref, other_ref, top_stack_ref, low_stack_ref, slab_hbm, updated_hbm, coupled_ref, sketch_next_ref,
+        for n in range(NEAR):
+            out_ref[k, n * width:(n + 1) * width] = sides[n][:width]
+        out_ref[k, NEAR * width:] = total[width:]
+
+
+def update_kernel(scale, core_ref, mine_ref, other_ref, stack_ref, slab_hbm, updated_hbm, coupled_ref, sketch_next_ref,
                   slab_ref, updated_ref, blocks_ref, halves_ref, in_sems, out_sems):
     loads = start_loads(slab_hbm, slab_ref, in_sems)
     core = core_ref[0]
@@ -147,12 +151,11 @@
     pairs = blocks_ref.shape[1] // PAIR
     pieces = mine_ref.shape[0]
     per = half * pairs // pieces
-    tall = (mine_ref.shape[1] - per) // blocks
     for ref, owner in ((mine_ref, core), (other_ref, 1 - core)):
         for t in range(half):
             for i in range(pairs):
                 k, place = divmod(t * pairs + i, per)
-                blocks_ref[owner * half + t, PAIR * i:PAIR * (i + 1), :] = ref[k, tall * blocks + place]
+                blocks_ref[owner * half + t, PAIR * i:PAIR * (i + 1), :] = ref[k, NEAR * blocks + place]
     panel_sketch = jnp.concatenate([blocks_ref[j, panel:, :] for j in range(blocks)], axis=0)
     gram = contract(panel_sketch, panel_sketch, 1, 1, HIGHEST)
     row = lax.broadcasted_iota(jnp.int32, gram.shape, 0)
@@ -173,12 +176,10 @@
     high, low = parts_of(coupled)
     right = jnp.concatenate([high, high, low], axis=0)
     step = slab_ref.shape[0] // CHUNKS
-    part = CHUNKS // 2
     stores = []
     for k in range(CHUNKS):
         rows = pl.ds(k * step, step)
-        stack_ref = (top_stack_ref, low_stack_ref)[k // part]
-        moved = contract(stack_ref[(k % part) * step:(k % part + 1) * step, :], right, 1, 0)
+        moved = contract(stack_ref[k * step:(k + 1) * step, :], right, 1, 0)
         loads[k].wait()
         updated_ref[k * step:(k + 1) * step, :] = slab_ref[k * step:(k + 1) * step, :] - moved
         stores.append(pltpu.make_async_copy(updated_ref.at[rows, :], updated_hbm.at[rows, :], out_sems.at[k]))
@@ -186,10 +187,10 @@
     count = sketch_rows // CORES
     for ref, owner in ((mine_ref, core), (other_ref, 1 - core)):
         for k in range(pieces):
-            for p in range(tall):
-                first = (k * tall + p) * PAIR
+            for n in range(NEAR):
+                first = n * count // NEAR + PAIR * k
                 for j in range(blocks):
-                    halves_ref[owner, first:first + PAIR, j * LANES:(j + 1) * LANES] = ref[k, p * blocks + j]
+                    halves_ref[owner, first:first + PAIR, j * LANES:(j + 1) * LANES] = ref[k, n * blocks + j]
     correction = contract(panel_sketch, coupled, 0, 0, HIGHEST)
     for c in range(CORES):
         span = slice(c * count, (c + 1) * count)
@@ -201,12 +202,13 @@
 def local(slab, reflectors, sketch):
     depth, columns = slab.shape
     sketch_rows = sketch.shape[0]
-    cols, lines = lax.axis_size("col"), lax.axis_size("z")
+    cols, lines = lax.axis_size("col"), lax.axis_size("far") * NEAR
+    z = ("far", "near")
     own = reflectors.shape[1]
     panel = own * cols
     total_rows = depth * lines * CORES
     blocks = columns // LANES
-    core = lax.axis_index("core").astype(jnp.int32).reshape(1)
+    core, near = (lax.axis_index(name).astype(jnp.int32).reshape(1) for name in ("core", "near"))
     vmem, smem, free = (pl.BlockSpec(memory_space=space) for space in (pltpu.VMEM, pltpu.SMEM, pl.ANY))
     f32, bf16 = jnp.float32, jnp.bfloat16
 
@@ -224,16 +226,19 @@
     whole = pltpu.VMEM((depth, columns), f32)
     slab_bytes = depth * columns * 4
 
-    spread = call(spread_kernel, "spread", (cols, own, depth), [vmem], grant=ALL_VMEM)(reflectors.T)
+    spread = call(spread_kernel, "spread", (cols, own, depth), [vmem], moved=4 * slab_bytes, grant=ALL_VMEM)(reflectors.T)
     gathered = lax.all_to_all(spread, "col", 0, 0, tiled=True)
 
     half_rows = sketch_rows // CORES
     sketch_half = (half_rows // PAIR, blocks, PAIR, LANES)
+    sketch_quarter = (half_rows // PAIR // NEAR, blocks, PAIR, LANES)
     mine_sketch, other_sketch, high, low = call(
         sketch_slab_kernel, "sketch_slab", [sketch_half, sketch_half, slab.shape, slab.shape], [smem, vmem, vmem], [vmem] * 4,
         [pltpu.VMEM((CORES, half_rows, columns), f32)],
         flops=6 * sketch_rows * depth * columns, moved=2 * slab_bytes, grant=MIDDLE_VMEM, dtypes=[f32, f32, bf16, bf16])(core, sketch, slab)
-    got_sketch = lax.ppermute(other_sketch, "core", SWAP)
+    got = lax.ppermute(other_sketch, "core", SWAP)
+    keep, send = call(split_kernel, "add_sketch", [sketch_quarter] * 2, [smem, vmem, vmem], [vmem, vmem])(near, mine_sketch, got)
+    got_sketch = lax.ppermute(send, "near", SWAP)
 
     rows = panel + panel // blocks
     pairs = blocks // CORES * rows // PAIR
@@ -244,38 +249,32 @@
             [pltpu.VMEM((panel, depth), f32)],
             flops=3 * panel * depth * columns, moved=slab_bytes, grant=MIDDLE_VMEM)(core, gathered, sketch, high, low, after)
 
-    def stack(first, after):
-        count = depth // 2
-        return call(
-            lambda *refs: stack_kernel(first, *refs), "panel_parts", (count, 3 * panel), [free, vmem],
-            scratch=[pltpu.VMEM((panel, count), f32)], flops=100 * panel * count, moved=panel * count * 10, dtypes=bf16)(after, gathered)
-
-    other = products(False, core)
+    other = products(False, send)
     got = lax.ppermute(other, "core", SWAP)
     mine = products(True, other)
+    stack = call(
+        stack_kernel, "panel_parts", (depth, 3 * panel), [free, vmem], scratch=[pltpu.VMEM((panel, depth), f32)],
+        flops=100 * panel * depth, moved=panel * depth * 10, dtypes=bf16)(mine, gathered)
     per = pairs // lines
-    width = half_rows // PAIR // lines * blocks + per
-    sums = call(join_kernel, "join", (lines, width, PAIR, LANES), [vmem] * 4)(mine_sketch, got_sketch, mine, got)
-    parts = lax.all_to_all(sums, "z", 0, 0, tiled=True)
-    top_stack = stack(0, sums)
-    summed = call(sum_kernel, "sum_parts", parts.shape, [vmem, free])(parts, top_stack)
-    whole_sums = lax.all_to_all(summed, "z", 0, 0, tiled=True)
-    low_stack = stack(depth // 2, summed)
-    mine = call(pass_kernel, "pass_on", summed.shape, [vmem, free])(whole_sums, low_stack)
+    sums = call(join_kernel, "join", (lines, blocks + per, PAIR, LANES), [vmem] * 4 + [free])(keep, got_sketch, mine, got, stack)
+    parts = lax.all_to_all(sums, z, 0, 0, tiled=True)
+    summed = call(
+        lambda *refs: sum_kernel(blocks, *refs), "sum_parts", (lines, NEAR * blocks + per, PAIR, LANES), [vmem])(parts)
+    mine = lax.all_to_all(summed, z, 0, 0, tiled=True)
     other = lax.ppermute(mine, "core", SWAP)
 
     scale = (sketch_rows / total_rows) ** 0.5
     updated, coupled, sketch_next = call(
         lambda *refs: update_kernel(scale, *refs), "solve_update", [slab.shape, (panel, columns), (sketch_rows, columns)],
-        [smem] + [vmem] * 4 + [free], [free, vmem, vmem],
+        [smem] + [vmem] * 3 + [free], [free, vmem, vmem],
         [whole, whole, pltpu.VMEM((blocks, rows, LANES), f32), pltpu.VMEM((CORES, half_rows, columns), f32), dma, dma],
-        flops=6 * panel * depth * columns, moved=2 * slab_bytes, grant=LARGE_VMEM)(core, mine, other, top_stack, low_stack, slab)
+        flops=6 * panel * depth * columns, moved=2 * slab_bytes, grant=LARGE_VMEM)(core, mine, other, stack, slab)
     return (updated, coupled, sketch_next)
 
 
 def solution(mesh):
-    split = Mesh(mesh.devices.reshape(-1, CORES, mesh.devices.shape[1]), ("z", "core", "col"))
-    row = ("z", "core")
+    split = Mesh(mesh.devices.reshape(-1, NEAR, CORES, mesh.devices.shape[1]), ("far", "near", "core", "col"))
+    row = ("far", "near", "core")
     in_specs = (P(row, "col"), P(row, "col"), P(None, row))
     out_specs = (P(row, "col"), P(None, "col"), P(None, "col"))
     return jax.shard_map(local, mesh=split, in_specs=in_specs, out_specs=out_specs, check_vma=False)

time: 86.4 us -> 86.1 us (level)
  blocking collectives: 0 us -> 44.2 us
  waiting for transfers between devices: 26.8 us -> 4.98 us
  starting transfers between devices: 46.6 us -> 25.5 us
  Pallas kernels: 9.01 us -> 7.56 us
    all_to_all x0 -> x2, blocking collectives: none -> 44.2 us  [the longest x1 25 us: local(): parts = lax.all_to_all(sums, z, 0, 0, tiled=True)]
    all_to_all x2 -> x0, waiting for transfers between devices: 25.4 us -> none  [the longest x1 12.9 us: local(): parts = lax.all_to_all(sums, 'z', 0, 0, tiled=True)]
    all_to_all x2 -> x0, starting transfers between devices: 22.1 us -> none  [the longest x1 13.1 us: local(): parts = lax.all_to_all(sums, 'z', 0, 0, tiled=True)]
    ppermute x1 -> x2, waiting for transfers between devices: 0.01 us -> 3.9 us  [the longest x1 2.94 us: local(): got_sketch = lax.ppermute(send, 'near', SWAP)]
    ppermute x1 -> x2, starting transfers between devices: 4.74 us -> 6.66 us  [the longest x1 4.74 us: local(): got = lax.ppermute(other_sketch, 'core', SWAP)]
    pallas_call x6 -> x5, Pallas kernels: 3.37 us -> 1.93 us  [the longest x1 1.5 us: local(): call(spread_kernel, 'spread', (cols, own, depth), [vmem], moved=4 * slab_...]
    ppermute x1, starting transfers between devices: 4.98 us -> 3.95 us  [local(): got = lax.ppermute(other, 'core', SWAP)]
  transfers between devices with their start and end apart: 6 -> 5, of which waited for: 4 -> 3; matrix products, arithmetic and copies ran while one was open for 0% -> 0% of each run, Pallas kernels for 2% -> 2%
where the time goes in v4:
time: 86.1 us; the launch traced here: 85.6 us
  blocking collectives  44.2 us (51%)
  starting transfers between devices  25.5 us (30%)
  Pallas kernels  7.56 us (9%)
  waiting for transfers between devices  4.98 us (6%)
  local copies, waits for them, and re-layouts  2.63 us (3%)
    all_to_all x1, blocking collectives, local(): parts = lax.all_to_all(sums, z, 0, 0, tiled=True)  25 us
    all_to_all x1, blocking collectives, local(): mine = lax.all_to_all(summed, z, 0, 0, tiled=True)  19.2 us
    all_to_all x1, starting transfers between devices, local(): gathered = lax.all_to_all(spread, 'col', 0, 0, tiled=True)  7.58 us
    ppermute x1, starting transfers between devices, local(): other = lax.ppermute(mine, 'core', SWAP)  7.34 us
    ppermute x1, starting transfers between devices, local(): got = lax.ppermute(other_sketch, 'core', SWAP)  4.74 us
    ppermute x1, starting transfers between devices, local(): got = lax.ppermute(other, 'core', SWAP)  3.95 us
    pallas_call x1, Pallas kernels, local(): call(lambda *refs: update_kernel(scale, *refs), 'solve_update', [slab.sha...  3.87 us
    ppermute x1, waiting for transfers between devices, local(): got_sketch = lax.ppermute(send, 'near', SWAP)  2.94 us
  transfers between devices with their start and end apart: 5, of which 3 were waited for; matrix products, arithmetic and copies ran while one was open for 0% of the time, Pallas kernels for 2%

profile of v4, /device:TPU:1, one launch (start us, length us, event | category | flops | bytes accessed | tf_op | source)
XLA Modules:
  0.0 85.6 jit_solution(2162811683612135541)
XLA Ops:
  0.6 0.0 copy-start.2
  0.6 1.5 %spread.1 = f32[16,4,1024]{2,1,0:T(4,128)} custom-call(f32[4,1024]{1,0:T(4,128)} %bitcast.3), custom_call_target="tpu_custom_call" | custom-call | bytes 8388608 | tf_op jit(solution)/shard_map/spread/pallas_call | solution.py:229
  2.1 7.6 %all-to-all-start = ((f32[16,4,1024]{2,1,0:T(4,128)}), f32[16,4,1024]{2,1,0:T(4,128)S(1)}, u32[]{:S(2)}, u32[]{:S(2)}) async-start(f32[16,4,1024]{2,1,0:T(4,128)} %spread.1), calls=%async_computation | async-start | bytes 524288 | tf_op jit(solution)/shard_map/all_to_all | solution.py:230
  9.7 0.0 copy-start
  9.7 1.6 %copy-done = f32[1024,512]{1,0:T(8,128)S(1)} copy-done((f32[1024,512]{1,0:T(8,128)S(1)}, f32[1024,512]{1,0:T(8,128)}, u32[]{:S(2)}) %copy-start) | copy-done | bytes 2097176
  11.3 0.0 copy-start.1
  11.3 1.0 %copy-done.1 = f32[128,1024]{1,0:T(8,128)S(1)} copy-done((f32[128,1024]{1,0:T(8,128)S(1)}, f32[128,1024]{1,0:T(8,128)}, u32[]{:S(2)}) %copy-start.1) | copy-done | bytes 524312
  12.4 0.8 sketch_slab.1
  13.2 4.7 %collective-permute-start = (f32[32,4,2,128]{3,2,1,0:T(2,128)S(1)}, f32[32,4,2,128]{3,2,1,0:T(2,128)S(1)}, u32[]{:S(2)}, u32[]{:S(2)}) collective-permute-start(f32[32,4,2,128]{3,2,1,0:T(2,128)S(1)} %get-tuple-element.10), channel_id=1, source_target_pairs={{0,16},{16,0},{1,17},{17,1},{2,18},{18,2},{3,19},{19,3},{4,20},{20... | collective-permute-start | bytes 393224 | tf_op jit(solution)/shard_map/ppermute | solution.py:239
  17.9 1.0 %collective-permute-done.got_ref = f32[32,4,2,128]{3,2,1,0:T(2,128)S(1)} collective-permute-done((f32[32,4,2,128]{3,2,1,0:T(2,128)S(1)}, f32[32,4,2,128]{3,2,1,0:T(2,128)S(1)}, u32[]{:S(2)}, u32[]{:S(2)}) %collective-permute-start) | collective-permute-done | bytes 131104 | tf_op jit(solution)/shard_map/ppermute | solution.py:239
  18.9 0.1 add_sketch.1
  19.0 0.0 all-to-all-done.refs_1_.gathered_ref
  19.0 0.0 copy-done.2
  19.0 0.5 products.2.refs_5_
  19.5 3.9 %collective-permute-start.2 = (f32[80,2,128]{2,1,0:T(2,128)S(1)}, f32[80,2,128]{2,1,0:T(2,128)S(1)}, u32[]{:S(2)}, u32[]{:S(2)}) collective-permute-start(f32[80,2,128]{2,1,0:T(2,128)S(1)} %products.2.refs_5_), channel_id=1, source_target_pairs={{0,16},{16,0},{1,17},{17,1},{2,18},{18,2},{3,19},{19,3},{4,20},{20... | collective-permute-start | bytes 245768 | tf_op jit(solution)/shard_map/ppermute | solution.py:253
  23.4 1.9 %collective-permute-start.1 = (f32[16,4,2,128]{3,2,1,0:T(2,128)S(1)}, f32[16,4,2,128]{3,2,1,0:T(2,128)S(1)}, u32[]{:S(2)}, u32[]{:S(2)}) collective-permute-start(f32[16,4,2,128]{3,2,1,0:T(2,128)S(1)} %get-tuple-element.12.refs_5_), channel_id=1, source_target_pairs={{0,32},{32,0},{1,33},{33,1},{2,34},{34,2},{3,35},{35,3},{4,36},{36... | collective-permute-start | bytes 196616 | tf_op jit(solution)/shard_map/ppermute | solution.py:241
  25.3 0.5 products.3.after_ref.mine_ref
  25.8 0.2 panel_parts.1.after_ref.refs_3_
  26.1 2.9 %collective-permute-done.1.got_sketch_ref = f32[16,4,2,128]{3,2,1,0:T(2,128)S(1)} collective-permute-done((f32[16,4,2,128]{3,2,1,0:T(2,128)S(1)}, f32[16,4,2,128]{3,2,1,0:T(2,128)S(1)}, u32[]{:S(2)}, u32[]{:S(2)}) %collective-permute-start.1) | collective-permute-done | bytes 65568 | tf_op jit(solution)/shard_map/ppermute | solution.py:241
  29.0 0.0 collective-permute-done.2.got_ref
  29.0 0.1 join.1
  29.1 25.0 %all_to_all.15.refs_0_ = f32[16,9,2,128]{3,2,1,0:T(2,128)S(1)} all-to-all(f32[16,9,2,128]{3,2,1,0:T(2,128)S(1)} %join.1), channel_id=1, replica_groups=mesh['far'=8,'near'=2,'core'=2,'col'=16] {'far','near'}, dimensions={0} | all-to-all | bytes 294912 | tf_op jit(solution)/shard_map/all_to_all | solution.py:260
  54.1 0.1 sum_parts.1
  54.2 19.2 %all_to_all.16.refs_1_ = f32[16,13,2,128]{3,2,1,0:T(2,128)S(1)} all-to-all(f32[16,13,2,128]{3,2,1,0:T(2,128)S(1)} %sum_parts.1), channel_id=1, replica_groups=mesh['far'=8,'near'=2,'core'=2,'col'=16] {'far','near'}, dimensions={0} | all-to-all | bytes 425984 | tf_op jit(solution)/shard_map/all_to_all | solution.py:263
  73.4 7.3 %collective-permute-start.3 = (f32[16,13,2,128]{3,2,1,0:T(2,128)S(1)}, f32[16,13,2,128]{3,2,1,0:T(2,128)S(1)}, u32[]{:S(2)}, u32[]{:S(2)}) collective-permute-start(f32[16,13,2,128]{3,2,1,0:T(2,128)S(1)} %all_to_all.16.refs_1_), channel_id=1, source_target_pairs={{0,16},{16,0},{1,17},{17,1},{2,18},{18,2},{3,19},{19,3},{4,20},{20... | collective-permute-start | bytes 638984 | tf_op jit(solution)/shard_map/ppermute | solution.py:264
  80.7 1.1 %collective-permute-done.3.refs_2_ = f32[16,13,2,128]{3,2,1,0:T(2,128)S(1)} collective-permute-done((f32[16,13,2,128]{3,2,1,0:T(2,128)S(1)}, f32[16,13,2,128]{3,2,1,0:T(2,128)S(1)}, u32[]{:S(2)}, u32[]{:S(2)}) %collective-permute-start.3) | collective-permute-done | bytes 213024 | tf_op jit(solution)/shard_map/ppermute | solution.py:264
  81.8 3.9 %solve_update.1 = (f32[1024,512]{1,0:T(8,128)}, f32[64,512]{1,0:T(8,128)}, f32[128,512]{1,0:T(8,128)}) custom-call(s32[1]{0:T(128)} %bitcast.core_ref.refs_0_, f32[16,13,2,128]{3,2,1,0:T(2,128)S(1)} %all_to_all.16.refs_1_, f32[16,13,2,128]{3,2,1,0:T(2,128)S(1)} %collective-permute-done.3.refs_2_, bf16[1024,192]{1,0:T(8,128)(2,1)S(1)} %panel_parts.1.after_ref.refs_3_, ...), custom_call_target="tpu_custom_call" | custom-call | flops 201326592 | bytes 4194304 | tf_op jit(solution)/shard_map/solve_update/pallas_call | solution.py:267
Async XLA Ops:
  0.6 18.3 %copy-start.2 = (f32[128,1024]{1,0:T(8,128)S(1)}, f32[128,1024]{1,0:T(8,128)}, u32[]{:S(2)}) copy-start(f32[128,1024]{1,0:T(8,128)} %refs_2_.3) | copy-start | bytes 1572868
  2.1 16.8 %all-to-all-start = ((f32[16,4,1024]{2,1,0:T(4,128)}), f32[16,4,1024]{2,1,0:T(4,128)S(1)}, u32[]{:S(2)}, u32[]{:S(2)}) async-start(f32[16,4,1024]{2,1,0:T(4,128)} %spread.1), calls=%async_computation | async-start | bytes 524288 | tf_op jit(solution)/shard_map/all_to_all | solution.py:230
  9.7 1.6 %copy-start = (f32[1024,512]{1,0:T(8,128)S(1)}, f32[1024,512]{1,0:T(8,128)}, u32[]{:S(2)}) copy-start(f32[1024,512]{1,0:T(8,128)} %refs_4_.1) | copy-start | bytes 6291460
  11.3 1.0 %copy-start.1 = (f32[128,1024]{1,0:T(8,128)S(1)}, f32[128,1024]{1,0:T(8,128)}, u32[]{:S(2)}) copy-start(f32[128,1024]{1,0:T(8,128)} %refs_2_.3) | copy-start | bytes 1572868
  13.2 5.7 %collective-permute-start = (f32[32,4,2,128]{3,2,1,0:T(2,128)S(1)}, f32[32,4,2,128]{3,2,1,0:T(2,128)S(1)}, u32[]{:S(2)}, u32[]{:S(2)}) collective-permute-start(f32[32,4,2,128]{3,2,1,0:T(2,128)S(1)} %get-tuple-element.10), channel_id=1, source_target_pairs={{0,16},{16,0},{1,17},{17,1},{2,18},{18,2},{3,19},{19,3},{4,20},{20... | collective-permute-start | bytes 393224 | tf_op jit(solution)/shard_map/ppermute | solution.py:239
  19.5 9.6 %collective-permute-start.2 = (f32[80,2,128]{2,1,0:T(2,128)S(1)}, f32[80,2,128]{2,1,0:T(2,128)S(1)}, u32[]{:S(2)}, u32[]{:S(2)}) collective-permute-start(f32[80,2,128]{2,1,0:T(2,128)S(1)} %products.2.refs_5_), channel_id=1, source_target_pairs={{0,16},{16,0},{1,17},{17,1},{2,18},{18,2},{3,19},{19,3},{4,20},{20... | collective-permute-start | bytes 245768 | tf_op jit(solution)/shard_map/ppermute | solution.py:253
  23.4 5.6 %collective-permute-start.1 = (f32[16,4,2,128]{3,2,1,0:T(2,128)S(1)}, f32[16,4,2,128]{3,2,1,0:T(2,128)S(1)}, u32[]{:S(2)}, u32[]{:S(2)}) collective-permute-start(f32[16,4,2,128]{3,2,1,0:T(2,128)S(1)} %get-tuple-element.12.refs_5_), channel_id=1, source_target_pairs={{0,32},{32,0},{1,33},{33,1},{2,34},{34,2},{3,35},{35,3},{4,36},{36... | collective-permute-start | bytes 196616 | tf_op jit(solution)/shard_map/ppermute | solution.py:241
  73.4 8.4 %collective-permute-start.3 = (f32[16,13,2,128]{3,2,1,0:T(2,128)S(1)}, f32[16,13,2,128]{3,2,1,0:T(2,128)S(1)}, u32[]{:S(2)}, u32[]{:S(2)}) collective-permute-start(f32[16,13,2,128]{3,2,1,0:T(2,128)S(1)} %all_to_all.16.refs_1_), channel_id=1, source_target_pairs={{0,16},{16,0},{1,17},{17,1},{2,18},{18,2},{3,19},{19,3},{4,20},{20... | collective-permute-start | bytes 638984 | tf_op jit(solution)/shard_map/ppermute | solution.py:264

commit v5 on v3

--- a/solution.py
+++ b/solution.py
@@ -99,7 +99,8 @@
             out_ref[t * pairs + panel // PAIR + i] = panel_sketch[first:first + PAIR, :]
 
 
-def join_kernel(mine_sketch_ref, got_sketch_ref, mine_ref, got_ref, out_ref):
+def join_kernel(mine_sketch_ref, got_sketch_ref, mine_ref, got_ref, after_ref, out_ref):
+    del after_ref
     pieces = out_ref.shape[0]
     tall, blocks = mine_sketch_ref.shape[:2]
     tall = tall // pieces
@@ -111,19 +112,17 @@
         out_ref[k, tall * blocks:] = mine_ref[span] + got_ref[span]
 
 
-def stack_kernel(first, after_ref, gathered_ref, out_ref, panel_ref):
+def stack_kernel(after_ref, gathered_ref, out_ref, panel_ref):
     del after_ref
-    own = gathered_ref.shape[1]
-    count = out_ref.shape[0]
-    for k in range(gathered_ref.shape[0]):
-        panel_ref[k * own:(k + 1) * own, :] = gathered_ref[k, :, first:first + count]
-    value = panel_ref[...]
-    high = value.astype(jnp.bfloat16).astype(jnp.float32)
-    out_ref[...] = jnp.concatenate([high, value - high, high], axis=0).T.astype(jnp.bfloat16)
-
-
-def sum_kernel(parts_ref, after_ref, out_ref):
-    del after_ref
+    lay_panel(gathered_ref, panel_ref)
+    step = panel_ref.shape[1] // CHUNKS
+    for k in range(CHUNKS):
+        value = panel_ref[:, k * step:(k + 1) * step]
+        high = value.astype(jnp.bfloat16).astype(jnp.float32)
+        out_ref[k * step:(k + 1) * step, :] = jnp.concatenate([high, value - high, high], axis=0).T.astype(jnp.bfloat16)
+
+
+def sum_kernel(parts_ref, out_ref):
     total = parts_ref[0]
     for k in range(1, parts_ref.shape[0]):
         total = total + parts_ref[k]
@@ -131,12 +130,7 @@
         out_ref[k] = total
 
 
-def pass_kernel(value_ref, after_ref, out_ref):
-    del after_ref
-    out_ref[...] = value_ref[...]
-
-
-def update_kernel(scale, core_ref, mine_ref, other_ref, top_stack_ref, low_stack_ref, slab_hbm, updated_hbm, coupled_ref, sketch_next_ref,
+def update_kernel(scale, core_ref, mine_ref, other_ref, stack_ref, slab_hbm, updated_hbm, coupled_ref, sketch_next_ref,
                   slab_ref, updated_ref, blocks_ref, halves_ref, in_sems, out_sems):
     loads = start_loads(slab_hbm, slab_ref, in_sems)
     core = core_ref[0]
@@ -157,28 +151,26 @@
     gram = contract(panel_sketch, panel_sketch, 1, 1, HIGHEST)
     row = lax.broadcasted_iota(jnp.int32, gram.shape, 0)
     column = lax.broadcasted_iota(jnp.int32, gram.shape, 1)
-    strict = jnp.where(row > column, gram, 0.0)
-    diagonal = jnp.sum(jnp.where(row == column, gram, 0.0), axis=1, keepdims=True) * 0.5
-    inverse = 1.0 / diagonal
+    diagonal = jnp.where(row == column, gram, 0.0)
+    inverse = 1.0 / (jnp.sum(diagonal, axis=1, keepdims=True) * 0.5)
+    scaled = jnp.where(row > column, gram, 0.0) * (1.0 / (jnp.sum(diagonal, axis=0, keepdims=True) * 0.5))
     tiles = panel // 8
     values = [jnp.concatenate([blocks_ref[j, 8 * b:8 * b + 8, :] for j in range(blocks)], axis=1) for b in range(tiles)]
     scales = [jnp.broadcast_to(inverse[8 * b:8 * b + 8, :], (8, columns)) for b in range(tiles)]
     for i in range(panel):
         b, r = divmod(i, 8)
-        solved = values[b][r:r + 1, :] * scales[b][r:r + 1, :]
+        final = values[b][r:r + 1, :]
         for later in range(b, tiles):
-            values[later] = values[later] - strict[8 * later:8 * later + 8, i:i + 1] * solved
+            values[later] = values[later] - scaled[8 * later:8 * later + 8, i:i + 1] * final
     coupled = jnp.concatenate([values[b] * scales[b] for b in range(tiles)], axis=0)
     coupled_ref[...] = coupled
     high, low = parts_of(coupled)
     right = jnp.concatenate([high, high, low], axis=0)
     step = slab_ref.shape[0] // CHUNKS
-    part = CHUNKS // 2
     stores = []
     for k in range(CHUNKS):
         rows = pl.ds(k * step, step)
-        stack_ref = (top_stack_ref, low_stack_ref)[k // part]
-        moved = contract(stack_ref[(k % part) * step:(k % part + 1) * step, :], right, 1, 0)
+        moved = contract(stack_ref[k * step:(k + 1) * step, :], right, 1, 0)
         loads[k].wait()
         updated_ref[k * step:(k + 1) * step, :] = slab_ref[k * step:(k + 1) * step, :] - moved
         stores.append(pltpu.make_async_copy(updated_ref.at[rows, :], updated_hbm.at[rows, :], out_sems.at[k]))
@@ -224,7 +216,7 @@
     whole = pltpu.VMEM((depth, columns), f32)
     slab_bytes = depth * columns * 4
 
-    spread = call(spread_kernel, "spread", (cols, own, depth), [vmem], grant=ALL_VMEM)(reflectors.T)
+    spread = call(spread_kernel, "spread", (cols, own, depth), [vmem], moved=4 * slab_bytes, grant=ALL_VMEM)(reflectors.T)
     gathered = lax.all_to_all(spread, "col", 0, 0, tiled=True)
 
     half_rows = sketch_rows // CORES
@@ -244,32 +236,26 @@
             [pltpu.VMEM((panel, depth), f32)],
             flops=3 * panel * depth * columns, moved=slab_bytes, grant=MIDDLE_VMEM)(core, gathered, sketch, high, low, after)
 
-    def stack(first, after):
-        count = depth // 2
-        return call(
-            lambda *refs: stack_kernel(first, *refs), "panel_parts", (count, 3 * panel), [free, vmem],
-            scratch=[pltpu.VMEM((panel, count), f32)], flops=100 * panel * count, moved=panel * count * 10, dtypes=bf16)(after, gathered)
-
     other = products(False, core)
     got = lax.ppermute(other, "core", SWAP)
     mine = products(True, other)
+    stack = call(
+        stack_kernel, "panel_parts", (depth, 3 * panel), [free, vmem], scratch=[pltpu.VMEM((panel, depth), f32)],
+        flops=100 * panel * depth, moved=panel * depth * 10, dtypes=bf16)(mine, gathered)
     per = pairs // lines
     width = half_rows // PAIR // lines * blocks + per
-    sums = call(join_kernel, "join", (lines, width, PAIR, LANES), [vmem] * 4)(mine_sketch, got_sketch, mine, got)
+    sums = call(join_kernel, "join", (lines, width, PAIR, LANES), [vmem] * 4 + [free])(mine_sketch, got_sketch, mine, got, stack)
     parts = lax.all_to_all(sums, "z", 0, 0, tiled=True)
-    top_stack = stack(0, sums)
-    summed = call(sum_kernel, "sum_parts", parts.shape, [vmem, free])(parts, top_stack)
-    whole_sums = lax.all_to_all(summed, "z", 0, 0, tiled=True)
-    low_stack = stack(depth // 2, summed)
-    mine = call(pass_kernel, "pass_on", summed.shape, [vmem, free])(whole_sums, low_stack)
+    summed = call(sum_kernel, "sum_parts", parts.shape, [vmem])(parts)
+    mine = lax.all_to_all(summed, "z", 0, 0, tiled=True)
     other = lax.ppermute(mine, "core", SWAP)
 
     scale = (sketch_rows / total_rows) ** 0.5
     updated, coupled, sketch_next = call(
         lambda *refs: update_kernel(scale, *refs), "solve_update", [slab.shape, (panel, columns), (sketch_rows, columns)],
-        [smem] + [vmem] * 4 + [free], [free, vmem, vmem],
+        [smem] + [vmem] * 3 + [free], [free, vmem, vmem],
         [whole, whole, pltpu.VMEM((blocks, rows, LANES), f32), pltpu.VMEM((CORES, half_rows, columns), f32), dma, dma],
-        flops=6 * panel * depth * columns, moved=2 * slab_bytes, grant=LARGE_VMEM)(core, mine, other, top_stack, low_stack, slab)
+        flops=6 * panel * depth * columns, moved=2 * slab_bytes, grant=LARGE_VMEM)(core, mine, other, stack, slab)
     return (updated, coupled, sketch_next)
 
 

time: 86.4 us -> 84.3 us (0.976)
  blocking collectives: 0 us -> 47.3 us
  waiting for transfers between devices: 26.8 us -> 1.23 us
  starting transfers between devices: 46.6 us -> 24.5 us
  Pallas kernels: 9.01 us -> 7.44 us
    all_to_all x0 -> x2, blocking collectives: none -> 47.3 us  [the longest x1 26 us: local(): parts = lax.all_to_all(sums, 'z', 0, 0, tiled=True)]
    all_to_all x2 -> x0, waiting for transfers between devices: 25.4 us -> none  [the longest x1 12.9 us: local(): parts = lax.all_to_all(sums, 'z', 0, 0, tiled=True)]
    all_to_all x2 -> x0, starting transfers between devices: 22.1 us -> none  [the longest x1 13.1 us: local(): parts = lax.all_to_all(sums, 'z', 0, 0, tiled=True)]
    pallas_call x6 -> x4, Pallas kernels: 3.37 us -> 1.91 us  [the longest x1 1.5 us: local(): call(spread_kernel, 'spread', (cols, own, depth), [vmem], moved=4 * slab_...]
  transfers between devices with their start and end apart: 6 -> 4, of which waited for: 4 -> 2; matrix products, arithmetic and copies ran while one was open for 0% -> 0% of each run, Pallas kernels for 2% -> 2%
where the time goes in v5:
time: 84.3 us; the launch traced here: 83.9 us
  blocking collectives  47.3 us (56%)
  starting transfers between devices  24.5 us (29%)
  Pallas kernels  7.44 us (9%)
  local copies, waits for them, and re-layouts  2.63 us (3%)
  waiting for transfers between devices  1.23 us (1%)
    all_to_all x1, blocking collectives, local(): parts = lax.all_to_all(sums, 'z', 0, 0, tiled=True)  26 us
    all_to_all x1, blocking collectives, local(): mine = lax.all_to_all(summed, 'z', 0, 0, tiled=True)  21.3 us
    all_to_all x1, starting transfers between devices, local(): gathered = lax.all_to_all(spread, 'col', 0, 0, tiled=True)  7.58 us
    ppermute x1, starting transfers between devices, local(): other = lax.ppermute(mine, 'core', SWAP)  7.18 us
    ppermute x1, starting transfers between devices, local(): got = lax.ppermute(other, 'core', SWAP)  4.98 us
    ppermute x1, starting transfers between devices, local(): got_sketch = lax.ppermute(other_sketch, 'core', SWAP)  4.74 us
    pallas_call x1, Pallas kernels, local(): call(lambda *refs: update_kernel(scale, *refs), 'solve_update', [slab.sha...  3.77 us
    unnamed x6, local copies, waits for them, and re-layouts  2.63 us
  transfers between devices with their start and end apart: 4, of which 2 were waited for; matrix products, arithmetic and copies ran while one was open for 0% of the time, Pallas kernels for 2%

profile of v5, /device:TPU:1, one launch (start us, length us, event | category | flops | bytes accessed | tf_op | source)
XLA Modules:
  0.0 83.9 jit_solution(2289403682105267087)
XLA Ops:
  0.6 0.0 copy-start.2
  0.6 1.5 %spread.1 = f32[16,4,1024]{2,1,0:T(4,128)} custom-call(f32[4,1024]{1,0:T(4,128)} %bitcast.2), custom_call_target="tpu_custom_call" | custom-call | bytes 8388608 | tf_op jit(solution)/shard_map/spread/pallas_call | solution.py:219
  2.1 7.6 %all-to-all-start = ((f32[16,4,1024]{2,1,0:T(4,128)}), f32[16,4,1024]{2,1,0:T(4,128)S(1)}, u32[]{:S(2)}, u32[]{:S(2)}) async-start(f32[16,4,1024]{2,1,0:T(4,128)} %spread.1), calls=%async_computation | async-start | bytes 524288 | tf_op jit(solution)/shard_map/all_to_all | solution.py:220
  9.7 0.0 copy-start
  9.7 1.6 %copy-done = f32[1024,512]{1,0:T(8,128)S(1)} copy-done((f32[1024,512]{1,0:T(8,128)S(1)}, f32[1024,512]{1,0:T(8,128)}, u32[]{:S(2)}) %copy-start) | copy-done | bytes 2097176
  11.3 0.0 copy-start.1
  11.3 1.0 %copy-done.1 = f32[128,1024]{1,0:T(8,128)S(1)} copy-done((f32[128,1024]{1,0:T(8,128)S(1)}, f32[128,1024]{1,0:T(8,128)}, u32[]{:S(2)}) %copy-start.1) | copy-done | bytes 524312
  12.4 0.8 sketch_slab.1
  13.2 4.7 %collective-permute-start = (f32[32,4,2,128]{3,2,1,0:T(2,128)S(1)}, f32[32,4,2,128]{3,2,1,0:T(2,128)S(1)}, u32[]{:S(2)}, u32[]{:S(2)}) collective-permute-start(f32[32,4,2,128]{3,2,1,0:T(2,128)S(1)} %get-tuple-element.8), channel_id=1, source_target_pairs={{0,16},{16,0},{1,17},{17,1},{2,18},{18,2},{3,19},{19,3},{4,20},{20... | collective-permute-start | bytes 393224 | tf_op jit(solution)/shard_map/ppermute | solution.py:228
  17.9 0.0 all-to-all-done.refs_1_.gathered_ref
  17.9 0.0 copy-done.2
  18.0 0.5 products.2.refs_5_
  18.4 5.0 %collective-permute-start.1 = (f32[80,2,128]{2,1,0:T(2,128)S(1)}, f32[80,2,128]{2,1,0:T(2,128)S(1)}, u32[]{:S(2)}, u32[]{:S(2)}) collective-permute-start(f32[80,2,128]{2,1,0:T(2,128)S(1)} %products.2.refs_5_), channel_id=1, source_target_pairs={{0,16},{16,0},{1,17},{17,1},{2,18},{18,2},{3,19},{19,3},{4,20},{20... | collective-permute-start | bytes 245768 | tf_op jit(solution)/shard_map/ppermute | solution.py:240
  23.4 0.5 products.3.after_ref.mine_ref
  23.9 0.2 panel_parts.1.after_ref.refs_3_
  24.1 0.0 collective-permute-done.got_sketch_ref
  24.2 0.2 collective-permute-done.1.got_ref
  24.3 0.1 join.1
  24.4 26.0 %all_to_all.15.parts_ref = f32[16,13,2,128]{3,2,1,0:T(2,128)S(1)} all-to-all(f32[16,13,2,128]{3,2,1,0:T(2,128)S(1)} %join.1), channel_id=1, replica_groups=mesh['z'=16,'core'=2,'col'=16] {'z'}, dimensions={0} | all-to-all | bytes 425984 | tf_op jit(solution)/shard_map/all_to_all | solution.py:248
  50.4 0.1 sum_parts.1
  50.5 21.3 %all_to_all.16.refs_1_ = f32[16,13,2,128]{3,2,1,0:T(2,128)S(1)} all-to-all(f32[16,13,2,128]{3,2,1,0:T(2,128)S(1)} %sum_parts.1), channel_id=1, replica_groups=mesh['z'=16,'core'=2,'col'=16] {'z'}, dimensions={0} | all-to-all | bytes 425984 | tf_op jit(solution)/shard_map/all_to_all | solution.py:250
  71.9 7.2 %collective-permute-start.2 = (f32[16,13,2,128]{3,2,1,0:T(2,128)S(1)}, f32[16,13,2,128]{3,2,1,0:T(2,128)S(1)}, u32[]{:S(2)}, u32[]{:S(2)}) collective-permute-start(f32[16,13,2,128]{3,2,1,0:T(2,128)S(1)} %all_to_all.16.refs_1_), channel_id=1, source_target_pairs={{0,16},{16,0},{1,17},{17,1},{2,18},{18,2},{3,19},{19,3},{4,20},{20... | collective-permute-start | bytes 638984 | tf_op jit(solution)/shard_map/ppermute | solution.py:251
  79.0 1.1 %collective-permute-done.2.refs_2_ = f32[16,13,2,128]{3,2,1,0:T(2,128)S(1)} collective-permute-done((f32[16,13,2,128]{3,2,1,0:T(2,128)S(1)}, f32[16,13,2,128]{3,2,1,0:T(2,128)S(1)}, u32[]{:S(2)}, u32[]{:S(2)}) %collective-permute-start.2) | collective-permute-done | bytes 213024 | tf_op jit(solution)/shard_map/ppermute | solution.py:251
  80.1 3.8 %solve_update.1 = (f32[1024,512]{1,0:T(8,128)}, f32[64,512]{1,0:T(8,128)}, f32[128,512]{1,0:T(8,128)}) custom-call(s32[1]{0:T(128)} %bitcast.core_ref.refs_0_.refs_5_, f32[16,13,2,128]{3,2,1,0:T(2,128)S(1)} %all_to_all.16.refs_1_, f32[16,13,2,128]{3,2,1,0:T(2,128)S(1)} %collective-permute-done.2.refs_2_, bf16[1024,192]{1,0:T(8,128)(2,1)S(1)} %panel_parts.1.after_ref.refs_3_, ...), custom_call_target="tpu_custom_call" | custom-call | flops 201326592 | bytes 4194304 | tf_op jit(solution)/shard_map/solve_update/pallas_call | solution.py:254
Async XLA Ops:
  0.6 17.3 %copy-start.2 = (f32[128,1024]{1,0:T(8,128)S(1)}, f32[128,1024]{1,0:T(8,128)}, u32[]{:S(2)}) copy-start(f32[128,1024]{1,0:T(8,128)} %refs_2_.3) | copy-start | bytes 1572868
  2.1 15.8 %all-to-all-start = ((f32[16,4,1024]{2,1,0:T(4,128)}), f32[16,4,1024]{2,1,0:T(4,128)S(1)}, u32[]{:S(2)}, u32[]{:S(2)}) async-start(f32[16,4,1024]{2,1,0:T(4,128)} %spread.1), calls=%async_computation | async-start | bytes 524288 | tf_op jit(solution)/shard_map/all_to_all | solution.py:220
  9.7 1.6 %copy-start = (f32[1024,512]{1,0:T(8,128)S(1)}, f32[1024,512]{1,0:T(8,128)}, u32[]{:S(2)}) copy-start(f32[1024,512]{1,0:T(8,128)} %refs_4_.1) | copy-start | bytes 6291460
  11.3 1.0 %copy-start.1 = (f32[128,1024]{1,0:T(8,128)S(1)}, f32[128,1024]{1,0:T(8,128)}, u32[]{:S(2)}) copy-start(f32[128,1024]{1,0:T(8,128)} %refs_2_.3) | copy-start | bytes 1572868
  13.2 11.0 %collective-permute-start = (f32[32,4,2,128]{3,2,1,0:T(2,128)S(1)}, f32[32,4,2,128]{3,2,1,0:T(2,128)S(1)}, u32[]{:S(2)}, u32[]{:S(2)}) collective-permute-start(f32[32,4,2,128]{3,2,1,0:T(2,128)S(1)} %get-tuple-element.8), channel_id=1, source_target_pairs={{0,16},{16,0},{1,17},{17,1},{2,18},{18,2},{3,19},{19,3},{4,20},{20... | collective-permute-start | bytes 393224 | tf_op jit(solution)/shard_map/ppermute | solution.py:228
  18.4 5.9 %collective-permute-start.1 = (f32[80,2,128]{2,1,0:T(2,128)S(1)}, f32[80,2,128]{2,1,0:T(2,128)S(1)}, u32[]{:S(2)}, u32[]{:S(2)}) collective-permute-start(f32[80,2,128]{2,1,0:T(2,128)S(1)} %products.2.refs_5_), channel_id=1, source_target_pairs={{0,16},{16,0},{1,17},{17,1},{2,18},{18,2},{3,19},{19,3},{4,20},{20... | collective-permute-start | bytes 245768 | tf_op jit(solution)/shard_map/ppermute | solution.py:240
  71.9 8.3 %collective-permute-start.2 = (f32[16,13,2,128]{3,2,1,0:T(2,128)S(1)}, f32[16,13,2,128]{3,2,1,0:T(2,128)S(1)}, u32[]{:S(2)}, u32[]{:S(2)}) collective-permute-start(f32[16,13,2,128]{3,2,1,0:T(2,128)S(1)} %all_to_all.16.refs_1_), channel_id=1, source_target_pairs={{0,16},{16,0},{1,17},{17,1},{2,18},{18,2},{3,19},{19,3},{4,20},{20... | collective-permute-start | bytes 638984 | tf_op jit(solution)/shard_map/ppermute | solution.py:251

commit v6 on v4

--- a/solution.py
+++ b/solution.py
@@ -48,7 +48,7 @@
         out_ref[k] = own_ref[...]
 
 
-def sketch_slab_kernel(core_ref, sketch_ref, slab_ref, mine_ref, other_ref, high_ref, low_ref, halves_ref):
+def sketch_slab_kernel(near_ref, sketch_ref, slab_ref, mine_ref, other_ref, high_ref, low_ref, halves_ref):
     step = slab_ref.shape[0] // CHUNKS
     sketch_rows = sketch_ref.shape[0]
     sketch_high, sketch_low = parts_of(sketch_ref[...])
@@ -62,21 +62,26 @@
         wide = contract(both[:, rows], high, 1, 0)
         term = wide[:sketch_rows] + (wide[sketch_rows:] + contract(sketch_high[:, rows], low, 1, 0))
         total = term if total is None else total + term
-    half = sketch_rows // CORES
-    for c in range(CORES):
+    half = sketch_rows // NEAR
+    for c in range(NEAR):
         halves_ref[c] = total[c * half:(c + 1) * half, :]
-    core = core_ref[0]
-    for out, owner in ((other_ref, 1 - core), (mine_ref, core)):
+    near = near_ref[0]
+    for out, owner in ((other_ref, 1 - near), (mine_ref, near)):
         for p in range(out.shape[0]):
             for j in range(out.shape[1]):
                 out[p, j] = halves_ref[owner, PAIR * p:PAIR * (p + 1), j * LANES:(j + 1) * LANES]
 
 
-def split_kernel(near_ref, mine_ref, got_ref, keep_ref, send_ref):
-    near, count = near_ref[0], keep_ref.shape[0]
-    for out, side in ((send_ref, 1 - near), (keep_ref, near)):
-        span = pl.ds(side * count, count)
-        out[...] = mine_ref[span] + got_ref[span]
+def pack_kernel(core_ref, mine_sketch_ref, got_sketch_ref, other_ref, send_ref, keep_ref):
+    core = core_ref[0]
+    pieces, width = keep_ref.shape[:2]
+    per = other_ref.shape[0] // pieces
+    span = pl.ds(core * pieces, pieces)
+    keep_ref[...] = mine_sketch_ref[span] + got_sketch_ref[span]
+    first = (1 - core) * pieces
+    for k in range(pieces):
+        send_ref[k, :width] = mine_sketch_ref[first + k] + got_sketch_ref[first + k]
+        send_ref[k, width:] = other_ref[k * per:(k + 1) * per]
 
 
 def products_kernel(is_mine, core_ref, gathered_ref, sketch_ref, high_ref, low_ref, after_ref, out_ref, panel_ref):
@@ -107,14 +112,13 @@
             out_ref[t * pairs + panel // PAIR + i] = panel_sketch[first:first + PAIR, :]
 
 
-def join_kernel(keep_ref, got_sketch_ref, mine_ref, got_ref, after_ref, out_ref):
+def join_kernel(keep_ref, mine_ref, got_ref, after_ref, out_ref):
     del after_ref
     pieces, width = keep_ref.shape[:2]
     per = mine_ref.shape[0] // pieces
     for k in range(pieces):
-        out_ref[k, :width] = keep_ref[k] + got_sketch_ref[k]
-        span = slice(k * per, (k + 1) * per)
-        out_ref[k, width:] = mine_ref[span] + got_ref[span]
+        out_ref[k, :width] = keep_ref[k] + got_ref[k, :width]
+        out_ref[k, width:] = mine_ref[k * per:(k + 1) * per] + got_ref[k, width:]
 
 
 def stack_kernel(after_ref, gathered_ref, out_ref, panel_ref):
@@ -160,17 +164,17 @@
     gram = contract(panel_sketch, panel_sketch, 1, 1, HIGHEST)
     row = lax.broadcasted_iota(jnp.int32, gram.shape, 0)
     column = lax.broadcasted_iota(jnp.int32, gram.shape, 1)
-    strict = jnp.where(row > column, gram, 0.0)
-    diagonal = jnp.sum(jnp.where(row == column, gram, 0.0), axis=1, keepdims=True) * 0.5
-    inverse = 1.0 / diagonal
+    diagonal = jnp.where(row == column, gram, 0.0)
+    inverse = 1.0 / (jnp.sum(diagonal, axis=1, keepdims=True) * 0.5)
+    scaled = jnp.where(row > column, gram, 0.0) * (1.0 / (jnp.sum(diagonal, axis=0, keepdims=True) * 0.5))
     tiles = panel // 8
     values = [jnp.concatenate([blocks_ref[j, 8 * b:8 * b + 8, :] for j in range(blocks)], axis=1) for b in range(tiles)]
     scales = [jnp.broadcast_to(inverse[8 * b:8 * b + 8, :], (8, columns)) for b in range(tiles)]
     for i in range(panel):
         b, r = divmod(i, 8)
-        solved = values[b][r:r + 1, :] * scales[b][r:r + 1, :]
+        final = values[b][r:r + 1, :]
         for later in range(b, tiles):
-            values[later] = values[later] - strict[8 * later:8 * later + 8, i:i + 1] * solved
+            values[later] = values[later] - scaled[8 * later:8 * later + 8, i:i + 1] * final
     coupled = jnp.concatenate([values[b] * scales[b] for b in range(tiles)], axis=0)
     coupled_ref[...] = coupled
     high, low = parts_of(coupled)
@@ -192,9 +196,11 @@
                 for j in range(blocks):
                     halves_ref[owner, first:first + PAIR, j * LANES:(j + 1) * LANES] = ref[k, n * blocks + j]
     correction = contract(panel_sketch, coupled, 0, 0, HIGHEST)
+    share = count // NEAR
     for c in range(CORES):
-        span = slice(c * count, (c + 1) * count)
-        sketch_next_ref[span, :] = (halves_ref[c] - correction[span, :]) * scale
+        for n in range(NEAR):
+            span = slice((n * CORES + c) * share, (n * CORES + c + 1) * share)
+            sketch_next_ref[span, :] = (halves_ref[c, n * share:(n + 1) * share, :] - correction[span, :]) * scale
     for copy in stores:
         copy.wait()
 
@@ -234,11 +240,9 @@
     sketch_quarter = (half_rows // PAIR // NEAR, blocks, PAIR, LANES)
     mine_sketch, other_sketch, high, low = call(
         sketch_slab_kernel, "sketch_slab", [sketch_half, sketch_half, slab.shape, slab.shape], [smem, vmem, vmem], [vmem] * 4,
-        [pltpu.VMEM((CORES, half_rows, columns), f32)],
-        flops=6 * sketch_rows * depth * columns, moved=2 * slab_bytes, grant=MIDDLE_VMEM, dtypes=[f32, f32, bf16, bf16])(core, sketch, slab)
-    got = lax.ppermute(other_sketch, "core", SWAP)
-    keep, send = call(split_kernel, "add_sketch", [sketch_quarter] * 2, [smem, vmem, vmem], [vmem, vmem])(near, mine_sketch, got)
-    got_sketch = lax.ppermute(send, "near", SWAP)
+        [pltpu.VMEM((NEAR, half_rows, columns), f32)],
+        flops=6 * sketch_rows * depth * columns, moved=2 * slab_bytes, grant=MIDDLE_VMEM, dtypes=[f32, f32, bf16, bf16])(near, sketch, slab)
+    got_sketch = lax.ppermute(other_sketch, "near", SWAP)
 
     rows = panel + panel // blocks
     pairs = blocks // CORES * rows // PAIR
@@ -249,14 +253,17 @@
             [pltpu.VMEM((panel, depth), f32)],
             flops=3 * panel * depth * columns, moved=slab_bytes, grant=MIDDLE_VMEM)(core, gathered, sketch, high, low, after)
 
-    other = products(False, send)
-    got = lax.ppermute(other, "core", SWAP)
-    mine = products(True, other)
+    other = products(False, core)
+    per = pairs // lines
+    send, keep = call(
+        pack_kernel, "pack", [(lines, blocks + per, PAIR, LANES), sketch_quarter], [smem, vmem, vmem, vmem], [vmem, vmem])(
+            core, mine_sketch, got_sketch, other)
+    got = lax.ppermute(send, "core", SWAP)
+    mine = products(True, send)
     stack = call(
         stack_kernel, "panel_parts", (depth, 3 * panel), [free, vmem], scratch=[pltpu.VMEM((panel, depth), f32)],
         flops=100 * panel * depth, moved=panel * depth * 10, dtypes=bf16)(mine, gathered)
-    per = pairs // lines
-    sums = call(join_kernel, "join", (lines, blocks + per, PAIR, LANES), [vmem] * 4 + [free])(keep, got_sketch, mine, got, stack)
+    sums = call(join_kernel, "join", send.shape, [vmem] * 3 + [free])(keep, mine, got, stack)
     parts = lax.all_to_all(sums, z, 0, 0, tiled=True)
     summed = call(
         lambda *refs: sum_kernel(blocks, *refs), "sum_parts", (lines, NEAR * blocks + per, PAIR, LANES), [vmem])(parts)

time: 86.1 us -> 82.8 us (0.962)
  starting transfers between devices: 25.5 us -> 23.4 us
  waiting for transfers between devices: 4.98 us -> 3.48 us
    ppermute x3 -> x2, waiting for transfers between devices: 3.9 us -> 2.02 us  [the longest x1 1.77 us: local(): got_sketch = lax.ppermute(other_sketch, 'near', SWAP)]
    ppermute x3 -> x2, starting transfers between devices: 10.6 us -> 8.95 us  [the longest x1 5.4 us: local(): got = lax.ppermute(send, 'core', SWAP)]
  transfers between devices with their start and end apart: 5 -> 4, of which waited for: 3 -> 4; matrix products, arithmetic and copies ran while one was open for 0% -> 0% of each run, Pallas kernels for 2% -> 2%
where the time goes in v6:
time: 82.8 us; the launch traced here: 82.3 us
  blocking collectives  44.5 us (54%)
  starting transfers between devices  23.4 us (28%)
  Pallas kernels  7.46 us (9%)
  waiting for transfers between devices  3.48 us (4%)
  local copies, waits for them, and re-layouts  2.63 us (3%)
    all_to_all x1, blocking collectives, local(): parts = lax.all_to_all(sums, z, 0, 0, tiled=True)  25.1 us
    all_to_all x1, blocking collectives, local(): mine = lax.all_to_all(summed, z, 0, 0, tiled=True)  19.4 us
    all_to_all x1, starting transfers between devices, local(): gathered = lax.all_to_all(spread, 'col', 0, 0, tiled=True)  7.58 us
    ppermute x1, starting transfers between devices, local(): other = lax.ppermute(mine, 'core', SWAP)  6.89 us
    ppermute x1, starting transfers between devices, local(): got = lax.ppermute(send, 'core', SWAP)  5.4 us
    pallas_call x1, Pallas kernels, local(): call(lambda *refs: update_kernel(scale, *refs), 'solve_update', [slab.sha...  3.76 us
    ppermute x1, starting transfers between devices, local(): got_sketch = lax.ppermute(other_sketch, 'near', SWAP)  3.55 us
    unnamed x6, local copies, waits for them, and re-layouts  2.63 us
  transfers between devices with their start and end apart: 4, of which 4 were waited for; matrix products, arithmetic and copies ran while one was open for 0% of the time, Pallas kernels for 2%

profile of v6, /device:TPU:1, one launch (start us, length us, event | category | flops | bytes accessed | tf_op | source)
XLA Modules:
  0.0 82.3 jit_solution(18369096085071643453)
XLA Ops:
  0.6 0.0 copy-start.2
  0.6 1.5 %spread.1 = f32[16,4,1024]{2,1,0:T(4,128)} custom-call(f32[4,1024]{1,0:T(4,128)} %bitcast.3), custom_call_target="tpu_custom_call" | custom-call | bytes 8388608 | tf_op jit(solution)/shard_map/spread/pallas_call | solution.py:235
  2.1 7.6 %all-to-all-start = ((f32[16,4,1024]{2,1,0:T(4,128)}), f32[16,4,1024]{2,1,0:T(4,128)S(1)}, u32[]{:S(2)}, u32[]{:S(2)}) async-start(f32[16,4,1024]{2,1,0:T(4,128)} %spread.1), calls=%async_computation | async-start | bytes 524288 | tf_op jit(solution)/shard_map/all_to_all | solution.py:236
  9.7 0.0 copy-start
  9.7 1.6 %copy-done = f32[1024,512]{1,0:T(8,128)S(1)} copy-done((f32[1024,512]{1,0:T(8,128)S(1)}, f32[1024,512]{1,0:T(8,128)}, u32[]{:S(2)}) %copy-start) | copy-done | bytes 2097176
  11.3 0.0 copy-start.1
  11.3 1.0 %copy-done.1 = f32[128,1024]{1,0:T(8,128)S(1)} copy-done((f32[128,1024]{1,0:T(8,128)S(1)}, f32[128,1024]{1,0:T(8,128)}, u32[]{:S(2)}) %copy-start.1) | copy-done | bytes 524312
  12.4 0.8 sketch_slab.1
  13.2 3.5 %collective-permute-start = (f32[32,4,2,128]{3,2,1,0:T(2,128)S(1)}, f32[32,4,2,128]{3,2,1,0:T(2,128)S(1)}, u32[]{:S(2)}, u32[]{:S(2)}) collective-permute-start(f32[32,4,2,128]{3,2,1,0:T(2,128)S(1)} %get-tuple-element.10), channel_id=1, source_target_pairs={{0,32},{32,0},{1,33},{33,1},{2,34},{34,2},{3,35},{35,3},{4,36},{36... | collective-permute-start | bytes 393224 | tf_op jit(solution)/shard_map/ppermute | solution.py:245
  16.7 0.4 all-to-all-done.refs_1_.gathered_ref
  17.1 0.0 copy-done.2
  17.1 0.5 products.2.other_ref
  17.6 1.8 %collective-permute-done.got_sketch_ref = f32[32,4,2,128]{3,2,1,0:T(2,128)S(1)} collective-permute-done((f32[32,4,2,128]{3,2,1,0:T(2,128)S(1)}, f32[32,4,2,128]{3,2,1,0:T(2,128)S(1)}, u32[]{:S(2)}, u32[]{:S(2)}) %collective-permute-start) | collective-permute-done | bytes 131104 | tf_op jit(solution)/shard_map/ppermute | solution.py:245
  19.4 0.1 pack.1
  19.5 5.4 %collective-permute-start.1 = (f32[16,9,2,128]{3,2,1,0:T(2,128)S(1)}, f32[16,9,2,128]{3,2,1,0:T(2,128)S(1)}, u32[]{:S(2)}, u32[]{:S(2)}) collective-permute-start(f32[16,9,2,128]{3,2,1,0:T(2,128)S(1)} %get-tuple-element.14.refs_5_), channel_id=1, source_target_pairs={{0,16},{16,0},{1,17},{17,1},{2,18},{18,2},{3,19},{19,3},{4,20},{20... | collective-permute-start | bytes 442376 | tf_op jit(solution)/shard_map/ppermute | solution.py:261
  24.9 0.5 products.3.after_ref.mine_ref
  25.4 0.2 panel_parts.1.after_ref.refs_3_
  25.6 0.3 collective-permute-done.1.got_ref
  25.9 0.1 join.1
  25.9 25.1 %all_to_all.15.refs_0_ = f32[16,9,2,128]{3,2,1,0:T(2,128)S(1)} all-to-all(f32[16,9,2,128]{3,2,1,0:T(2,128)S(1)} %join.1), channel_id=1, replica_groups=mesh['far'=8,'near'=2,'core'=2,'col'=16] {'far','near'}, dimensions={0} | all-to-all | bytes 294912 | tf_op jit(solution)/shard_map/all_to_all | solution.py:267
  51.0 0.1 sum_parts.1
  51.1 19.4 %all_to_all.16.refs_1_ = f32[16,13,2,128]{3,2,1,0:T(2,128)S(1)} all-to-all(f32[16,13,2,128]{3,2,1,0:T(2,128)S(1)} %sum_parts.1), channel_id=1, replica_groups=mesh['far'=8,'near'=2,'core'=2,'col'=16] {'far','near'}, dimensions={0} | all-to-all | bytes 425984 | tf_op jit(solution)/shard_map/all_to_all | solution.py:270
  70.6 6.9 %collective-permute-start.2 = (f32[16,13,2,128]{3,2,1,0:T(2,128)S(1)}, f32[16,13,2,128]{3,2,1,0:T(2,128)S(1)}, u32[]{:S(2)}, u32[]{:S(2)}) collective-permute-start(f32[16,13,2,128]{3,2,1,0:T(2,128)S(1)} %all_to_all.16.refs_1_), channel_id=1, source_target_pairs={{0,16},{16,0},{1,17},{17,1},{2,18},{18,2},{3,19},{19,3},{4,20},{20... | collective-permute-start | bytes 638984 | tf_op jit(solution)/shard_map/ppermute | solution.py:271
  77.4 1.1 %collective-permute-done.2.refs_2_ = f32[16,13,2,128]{3,2,1,0:T(2,128)S(1)} collective-permute-done((f32[16,13,2,128]{3,2,1,0:T(2,128)S(1)}, f32[16,13,2,128]{3,2,1,0:T(2,128)S(1)}, u32[]{:S(2)}, u32[]{:S(2)}) %collective-permute-start.2) | collective-permute-done | bytes 213024 | tf_op jit(solution)/shard_map/ppermute | solution.py:271
  78.5 3.8 %solve_update.1 = (f32[1024,512]{1,0:T(8,128)}, f32[64,512]{1,0:T(8,128)}, f32[128,512]{1,0:T(8,128)}) custom-call(s32[1]{0:T(128)} %bitcast.refs_0_.refs_5_.core_ref, f32[16,13,2,128]{3,2,1,0:T(2,128)S(1)} %all_to_all.16.refs_1_, f32[16,13,2,128]{3,2,1,0:T(2,128)S(1)} %collective-permute-done.2.refs_2_, bf16[1024,192]{1,0:T(8,128)(2,1)S(1)} %panel_parts.1.after_ref.refs_3_, ...), custom_call_target="tpu_custom_call" | custom-call | flops 201326592 | bytes 4194304 | tf_op jit(solution)/shard_map/solve_update/pallas_call | solution.py:274
Async XLA Ops:
  0.6 16.5 %copy-start.2 = (f32[128,1024]{1,0:T(8,128)S(1)}, f32[128,1024]{1,0:T(8,128)}, u32[]{:S(2)}) copy-start(f32[128,1024]{1,0:T(8,128)} %refs_2_.3) | copy-start | bytes 1572868
  2.1 15.0 %all-to-all-start = ((f32[16,4,1024]{2,1,0:T(4,128)}), f32[16,4,1024]{2,1,0:T(4,128)S(1)}, u32[]{:S(2)}, u32[]{:S(2)}) async-start(f32[16,4,1024]{2,1,0:T(4,128)} %spread.1), calls=%async_computation | async-start | bytes 524288 | tf_op jit(solution)/shard_map/all_to_all | solution.py:236
  9.7 1.6 %copy-start = (f32[1024,512]{1,0:T(8,128)S(1)}, f32[1024,512]{1,0:T(8,128)}, u32[]{:S(2)}) copy-start(f32[1024,512]{1,0:T(8,128)} %refs_4_.1) | copy-start | bytes 6291460
  11.3 1.0 %copy-start.1 = (f32[128,1024]{1,0:T(8,128)S(1)}, f32[128,1024]{1,0:T(8,128)}, u32[]{:S(2)}) copy-start(f32[128,1024]{1,0:T(8,128)} %refs_2_.3) | copy-start | bytes 1572868
  13.2 6.2 %collective-permute-start = (f32[32,4,2,128]{3,2,1,0:T(2,128)S(1)}, f32[32,4,2,128]{3,2,1,0:T(2,128)S(1)}, u32[]{:S(2)}, u32[]{:S(2)}) collective-permute-start(f32[32,4,2,128]{3,2,1,0:T(2,128)S(1)} %get-tuple-element.10), channel_id=1, source_target_pairs={{0,32},{32,0},{1,33},{33,1},{2,34},{34,2},{3,35},{35,3},{4,36},{36... | collective-permute-start | bytes 393224 | tf_op jit(solution)/shard_map/ppermute | solution.py:245
  19.5 6.4 %collective-permute-start.1 = (f32[16,9,2,128]{3,2,1,0:T(2,128)S(1)}, f32[16,9,2,128]{3,2,1,0:T(2,128)S(1)}, u32[]{:S(2)}, u32[]{:S(2)}) collective-permute-start(f32[16,9,2,128]{3,2,1,0:T(2,128)S(1)} %get-tuple-element.14.refs_5_), channel_id=1, source_target_pairs={{0,16},{16,0},{1,17},{17,1},{2,18},{18,2},{3,19},{19,3},{4,20},{20... | collective-permute-start | bytes 442376 | tf_op jit(solution)/shard_map/ppermute | solution.py:261
  70.6 8.0 %collective-permute-start.2 = (f32[16,13,2,128]{3,2,1,0:T(2,128)S(1)}, f32[16,13,2,128]{3,2,1,0:T(2,128)S(1)}, u32[]{:S(2)}, u32[]{:S(2)}) collective-permute-start(f32[16,13,2,128]{3,2,1,0:T(2,128)S(1)} %all_to_all.16.refs_1_), channel_id=1, source_target_pairs={{0,16},{16,0},{1,17},{17,1},{2,18},{18,2},{3,19},{19,3},{4,20},{20... | collective-permute-start | bytes 638984 | tf_op jit(solution)/shard_map/ppermute | solution.py:271

commit v7 on v6

--- a/solution.py
+++ b/solution.py
@@ -43,9 +43,12 @@
         panel_ref[k * own:(k + 1) * own, :] = gathered_ref[k, :, :panel_ref.shape[1]]
 
 
-def spread_kernel(own_ref, out_ref):
-    for k in range(out_ref.shape[0]):
-        out_ref[k] = own_ref[...]
+def spread_kernel(own_ref, out_hbm, sems):
+    copies = [pltpu.make_async_copy(own_ref, out_hbm.at[k], sems.at[k]) for k in range(out_hbm.shape[0])]
+    for copy in copies:
+        copy.start()
+    for copy in copies:
+        copy.wait()
 
 
 def sketch_slab_kernel(near_ref, sketch_ref, slab_ref, mine_ref, other_ref, high_ref, low_ref, halves_ref):
@@ -232,7 +235,8 @@
     whole = pltpu.VMEM((depth, columns), f32)
     slab_bytes = depth * columns * 4
 
-    spread = call(spread_kernel, "spread", (cols, own, depth), [vmem], moved=4 * slab_bytes, grant=ALL_VMEM)(reflectors.T)
+    spread = call(spread_kernel, "spread", (cols, own, depth), [vmem], free, [pltpu.SemaphoreType.DMA((cols,))],
+                  moved=4 * slab_bytes, grant=ALL_VMEM)(reflectors.T)
     gathered = lax.all_to_all(spread, "col", 0, 0, tiled=True)
 
     half_rows = sketch_rows // CORES

time: 82.8 us -> 82.9 us (level)
  no operation moved by 1% of the time
where the time goes in v7:
time: 82.9 us; the launch traced here: 82.4 us
  blocking collectives  44.5 us (54%)
  starting transfers between devices  23.4 us (28%)
  Pallas kernels  7.57 us (9%)
  waiting for transfers between devices  3.48 us (4%)
  local copies, waits for them, and re-layouts  2.63 us (3%)
    all_to_all x1, blocking collectives, local(): parts = lax.all_to_all(sums, z, 0, 0, tiled=True)  25.1 us
    all_to_all x1, blocking collectives, local(): mine = lax.all_to_all(summed, z, 0, 0, tiled=True)  19.4 us
    all_to_all x1, starting transfers between devices, local(): gathered = lax.all_to_all(spread, 'col', 0, 0, tiled=True)  7.6 us
    ppermute x1, starting transfers between devices, local(): other = lax.ppermute(mine, 'core', SWAP)  6.89 us
    ppermute x1, starting transfers between devices, local(): got = lax.ppermute(send, 'core', SWAP)  5.41 us
    pallas_call x1, Pallas kernels, local(): call(lambda *refs: update_kernel(scale, *refs), 'solve_update', [slab.sha...  3.76 us
    ppermute x1, starting transfers between devices, local(): got_sketch = lax.ppermute(other_sketch, 'near', SWAP)  3.54 us
    unnamed x6, local copies, waits for them, and re-layouts  2.63 us
  transfers between devices with their start and end apart: 4, of which 4 were waited for; matrix products, arithmetic and copies ran while one was open for 0% of the time, Pallas kernels for 2%

profile of v7, /device:TPU:1, one launch (start us, length us, event | category | flops | bytes accessed | tf_op | source)
XLA Modules:
  0.0 82.4 jit_solution(4780058867140766201)
XLA Ops:
  0.6 0.0 copy-start.2
  0.6 1.6 %spread.1 = f32[16,4,1024]{2,1,0:T(4,128)} custom-call(f32[4,1024]{1,0:T(4,128)} %bitcast.3), custom_call_target="tpu_custom_call" | custom-call | bytes 8388608 | tf_op jit(solution)/shard_map/spread/pallas_call | solution.py:238
  2.2 7.6 %all-to-all-start = ((f32[16,4,1024]{2,1,0:T(4,128)}), f32[16,4,1024]{2,1,0:T(4,128)S(1)}, u32[]{:S(2)}, u32[]{:S(2)}) async-start(f32[16,4,1024]{2,1,0:T(4,128)} %spread.1), calls=%async_computation | async-start | bytes 524288 | tf_op jit(solution)/shard_map/all_to_all | solution.py:240
  9.9 0.0 copy-start
  9.9 1.6 %copy-done = f32[1024,512]{1,0:T(8,128)S(1)} copy-done((f32[1024,512]{1,0:T(8,128)S(1)}, f32[1024,512]{1,0:T(8,128)}, u32[]{:S(2)}) %copy-start) | copy-done | bytes 2097176
  11.5 0.0 copy-start.1
  11.5 1.0 %copy-done.1 = f32[128,1024]{1,0:T(8,128)S(1)} copy-done((f32[128,1024]{1,0:T(8,128)S(1)}, f32[128,1024]{1,0:T(8,128)}, u32[]{:S(2)}) %copy-start.1) | copy-done | bytes 524312
  12.5 0.8 sketch_slab.1
  13.3 3.5 %collective-permute-start = (f32[32,4,2,128]{3,2,1,0:T(2,128)S(1)}, f32[32,4,2,128]{3,2,1,0:T(2,128)S(1)}, u32[]{:S(2)}, u32[]{:S(2)}) collective-permute-start(f32[32,4,2,128]{3,2,1,0:T(2,128)S(1)} %get-tuple-element.10), channel_id=1, source_target_pairs={{0,32},{32,0},{1,33},{33,1},{2,34},{34,2},{3,35},{35,3},{4,36},{36... | collective-permute-start | bytes 393224 | tf_op jit(solution)/shard_map/ppermute | solution.py:249
  16.9 0.4 all-to-all-done.refs_1_.gathered_ref
  17.3 0.0 copy-done.2
  17.3 0.5 products.2.other_ref
  17.7 1.8 %collective-permute-done.got_sketch_ref = f32[32,4,2,128]{3,2,1,0:T(2,128)S(1)} collective-permute-done((f32[32,4,2,128]{3,2,1,0:T(2,128)S(1)}, f32[32,4,2,128]{3,2,1,0:T(2,128)S(1)}, u32[]{:S(2)}, u32[]{:S(2)}) %collective-permute-start) | collective-permute-done | bytes 131104 | tf_op jit(solution)/shard_map/ppermute | solution.py:249
  19.5 0.1 pack.1
  19.6 5.4 %collective-permute-start.1 = (f32[16,9,2,128]{3,2,1,0:T(2,128)S(1)}, f32[16,9,2,128]{3,2,1,0:T(2,128)S(1)}, u32[]{:S(2)}, u32[]{:S(2)}) collective-permute-start(f32[16,9,2,128]{3,2,1,0:T(2,128)S(1)} %get-tuple-element.14.refs_5_), channel_id=1, source_target_pairs={{0,16},{16,0},{1,17},{17,1},{2,18},{18,2},{3,19},{19,3},{4,20},{20... | collective-permute-start | bytes 442376 | tf_op jit(solution)/shard_map/ppermute | solution.py:265
  25.0 0.5 products.3.after_ref.mine_ref
  25.5 0.2 panel_parts.1.after_ref.refs_3_
  25.7 0.3 collective-permute-done.1.got_ref
  26.0 0.1 join.1
  26.1 25.1 %all_to_all.15.refs_0_ = f32[16,9,2,128]{3,2,1,0:T(2,128)S(1)} all-to-all(f32[16,9,2,128]{3,2,1,0:T(2,128)S(1)} %join.1), channel_id=1, replica_groups=mesh['far'=8,'near'=2,'core'=2,'col'=16] {'far','near'}, dimensions={0} | all-to-all | bytes 294912 | tf_op jit(solution)/shard_map/all_to_all | solution.py:271
  51.2 0.1 sum_parts.1
  51.2 19.4 %all_to_all.16.refs_1_ = f32[16,13,2,128]{3,2,1,0:T(2,128)S(1)} all-to-all(f32[16,13,2,128]{3,2,1,0:T(2,128)S(1)} %sum_parts.1), channel_id=1, replica_groups=mesh['far'=8,'near'=2,'core'=2,'col'=16] {'far','near'}, dimensions={0} | all-to-all | bytes 425984 | tf_op jit(solution)/shard_map/all_to_all | solution.py:274
  70.7 6.9 %collective-permute-start.2 = (f32[16,13,2,128]{3,2,1,0:T(2,128)S(1)}, f32[16,13,2,128]{3,2,1,0:T(2,128)S(1)}, u32[]{:S(2)}, u32[]{:S(2)}) collective-permute-start(f32[16,13,2,128]{3,2,1,0:T(2,128)S(1)} %all_to_all.16.refs_1_), channel_id=1, source_target_pairs={{0,16},{16,0},{1,17},{17,1},{2,18},{18,2},{3,19},{19,3},{4,20},{20... | collective-permute-start | bytes 638984 | tf_op jit(solution)/shard_map/ppermute | solution.py:275
  77.6 1.1 %collective-permute-done.2.refs_2_ = f32[16,13,2,128]{3,2,1,0:T(2,128)S(1)} collective-permute-done((f32[16,13,2,128]{3,2,1,0:T(2,128)S(1)}, f32[16,13,2,128]{3,2,1,0:T(2,128)S(1)}, u32[]{:S(2)}, u32[]{:S(2)}) %collective-permute-start.2) | collective-permute-done | bytes 213024 | tf_op jit(solution)/shard_map/ppermute | solution.py:275
  78.6 3.8 %solve_update.1 = (f32[1024,512]{1,0:T(8,128)}, f32[64,512]{1,0:T(8,128)}, f32[128,512]{1,0:T(8,128)}) custom-call(s32[1]{0:T(128)} %bitcast.refs_0_.refs_5_.core_ref, f32[16,13,2,128]{3,2,1,0:T(2,128)S(1)} %all_to_all.16.refs_1_, f32[16,13,2,128]{3,2,1,0:T(2,128)S(1)} %collective-permute-done.2.refs_2_, bf16[1024,192]{1,0:T(8,128)(2,1)S(1)} %panel_parts.1.after_ref.refs_3_, ...), custom_call_target="tpu_custom_call" | custom-call | flops 201326592 | bytes 4194304 | tf_op jit(solution)/shard_map/solve_update/pallas_call | solution.py:278
Async XLA Ops:
  0.6 16.6 %copy-start.2 = (f32[128,1024]{1,0:T(8,128)S(1)}, f32[128,1024]{1,0:T(8,128)}, u32[]{:S(2)}) copy-start(f32[128,1024]{1,0:T(8,128)} %refs_2_.3) | copy-start | bytes 1572868
  2.2 15.0 %all-to-all-start = ((f32[16,4,1024]{2,1,0:T(4,128)}), f32[16,4,1024]{2,1,0:T(4,128)S(1)}, u32[]{:S(2)}, u32[]{:S(2)}) async-start(f32[16,4,1024]{2,1,0:T(4,128)} %spread.1), calls=%async_computation | async-start | bytes 524288 | tf_op jit(solution)/shard_map/all_to_all | solution.py:240
  9.9 1.6 %copy-start = (f32[1024,512]{1,0:T(8,128)S(1)}, f32[1024,512]{1,0:T(8,128)}, u32[]{:S(2)}) copy-start(f32[1024,512]{1,0:T(8,128)} %refs_4_.1) | copy-start | bytes 6291460
  11.5 1.0 %copy-start.1 = (f32[128,1024]{1,0:T(8,128)S(1)}, f32[128,1024]{1,0:T(8,128)}, u32[]{:S(2)}) copy-start(f32[128,1024]{1,0:T(8,128)} %refs_2_.3) | copy-start | bytes 1572868
  13.3 6.2 %collective-permute-start = (f32[32,4,2,128]{3,2,1,0:T(2,128)S(1)}, f32[32,4,2,128]{3,2,1,0:T(2,128)S(1)}, u32[]{:S(2)}, u32[]{:S(2)}) collective-permute-start(f32[32,4,2,128]{3,2,1,0:T(2,128)S(1)} %get-tuple-element.10), channel_id=1, source_target_pairs={{0,32},{32,0},{1,33},{33,1},{2,34},{34,2},{3,35},{35,3},{4,36},{36... | collective-permute-start | bytes 393224 | tf_op jit(solution)/shard_map/ppermute | solution.py:249
  19.6 6.4 %collective-permute-start.1 = (f32[16,9,2,128]{3,2,1,0:T(2,128)S(1)}, f32[16,9,2,128]{3,2,1,0:T(2,128)S(1)}, u32[]{:S(2)}, u32[]{:S(2)}) collective-permute-start(f32[16,9,2,128]{3,2,1,0:T(2,128)S(1)} %get-tuple-element.14.refs_5_), channel_id=1, source_target_pairs={{0,16},{16,0},{1,17},{17,1},{2,18},{18,2},{3,19},{19,3},{4,20},{20... | collective-permute-start | bytes 442376 | tf_op jit(solution)/shard_map/ppermute | solution.py:265
  70.7 8.0 %collective-permute-start.2 = (f32[16,13,2,128]{3,2,1,0:T(2,128)S(1)}, f32[16,13,2,128]{3,2,1,0:T(2,128)S(1)}, u32[]{:S(2)}, u32[]{:S(2)}) collective-permute-start(f32[16,13,2,128]{3,2,1,0:T(2,128)S(1)} %all_to_all.16.refs_1_), channel_id=1, source_target_pairs={{0,16},{16,0},{1,17},{17,1},{2,18},{18,2},{3,19},{19,3},{4,20},{20... | collective-permute-start | bytes 638984 | tf_op jit(solution)/shard_map/ppermute | solution.py:275
